TPU v7x, 256 devices: a whole 4x4x8 slice. The times are simulated.
256 devices in a mesh: section: 16 (over x_hi, y, core), expert: 16 (over z, x_lo).
Axes of the slice: x: 4 (x_hi: 2, x_lo: 2; x = x_hi * 2 + x_lo), y: 4, z: 8, core: 2. Of those that a mesh axis runs over, the one named last changes fastest.
Arguments:
- forward_in: bfloat16 [16, 2048, 7168], P('section', 'expert'), may hold values from -6 to 6
- backward_saved: bfloat16 [16, 2048, 7168], P('section', 'expert'), may hold values from -6 to 6
- backward_grad: bfloat16 [16, 2048, 7168], P('section', 'expert'), may hold values from -6 to 6
- forward_routes: int32 [16, 2048, 2], P('section', 'expert'), may hold values from 0 to 127, as said below
- forward_gates: float32 [16, 2048, 2], P('section', 'expert'), may hold values from 0.2 to 1
- backward_routes: int32 [16, 2048, 2], P('section', 'expert'), may hold values from 0 to 127, as said below
- backward_gates: float32 [16, 2048, 2], P('section', 'expert'), may hold values from 0.2 to 1
- up_weight: bfloat16 [16, 7168, 2432], P('section', 'expert'), may hold values from -0.0625 to 0.0625
- down_weight: bfloat16 [16, 2432, 7168], P('section', None, 'expert'), may hold values from -0.125 to 0.125
Outputs:
- forward_out: bfloat16 [16, 2048, 7168], P('section', 'expert')
- backward_out: bfloat16 [16, 2048, 7168], P('section', 'expert')
Inputs may be any that keep to these rules, and one draw needn't show every extreme that they name: `forward_routes`: in every row the two ids differ. Of the 128 rows of one device (aligned blocks of a section), at most 17 name expert 0, and on some device exactly 17 do. `backward_routes`: in every row the two ids differ. Of the 128 rows of one device (aligned blocks of a section), at most 17 name expert 0, and on some device exactly 17 do.
All inputs are finite; a program needn't handle non-finite values.
Results may differ from a plain program's by a relative error of at most 0.005.
Values may be sent and summed in bfloat16 or wider, within the bound.
No kernel may reach another device: no remote copies, remote signals or barrier semaphores. Data moves between devices by JAX's collectives and lax.ppermute only.
A program may use at most 128 MiB of HBM per device.

v0:
```python
import functools

import jax
import jax.numpy as jnp
from jax import lax
from jax.experimental import pallas as pl
from jax.experimental.pallas import tpu as pltpu
from jax.sharding import PartitionSpec as P

MOST = 17
TOK = 128
D = 7168
FF = 2432
COLS = 448
NODES = 8
PICK = 56
CHUNK = 104
SENT = 72
ROWS = 24
FIRST = 1280
BF = jnp.bfloat16
F32 = jnp.float32
WIDE = 2 * COLS
VMEM_LIMIT = 48 * 1024 * 1024
VMEM_MOST = 60 * 1024 * 1024
STREAMS = (slice(0, FIRST), slice(FIRST, FF))
CUT = 48


def iota(shape, dim):
    return lax.broadcasted_iota(jnp.int32, shape, dim)


def dot(left, right):
    return jnp.dot(left, right, preferred_element_type=F32)


def dot_tn(left, right):
    return lax.dot_general(left, right, (((0,), (0,)), ((), ())), preferred_element_type=F32)


def dot_nt(left, right):
    return lax.dot_general(left, right, (((1,), (1,)), ((), ())), preferred_element_type=F32)


def onehot(cond):
    return jnp.where(cond, 1.0, 0.0).astype(BF)


def slot_rows(hit):
    wide = jnp.broadcast_to(hit, (TOK, TOK)).astype(BF)
    upto = onehot(iota((TOK, TOK), 0) <= iota((TOK, TOK), 1))
    return jnp.where(wide > 0.5, dot(wide, upto) - 1.0, -1.0)


def placed(slots, start):
    row = iota((PICK, TOK), 0) - start
    return (slots[:PICK] == row.astype(F32)) & (row >= 0)


def pick_kernel(froutes, fgates, broutes, bgates, acts, saved, cot, packed, meta, held, sems):
    sources = (acts, saved, cot)

    def strip(j):
        return pl.ds(pl.multiple_of(j * WIDE, TOK), WIDE)

    def fetch(j, i):
        return pltpu.make_async_copy(
            sources[i].at[:, strip(j)], held.at[i, :, strip(j)], sems.at[j, i]
        )

    @pl.loop(0, NODES)
    def _(j):
        for i in range(3):
            fetch(j, i).start()

    fhits, bhits = froutes[...] == 0, broutes[...] == 0
    fslots = slot_rows(jnp.sum(jnp.where(fhits, 1.0, 0.0), axis=0, keepdims=True))
    bslots = slot_rows(jnp.sum(jnp.where(bhits, 1.0, 0.0), axis=0, keepdims=True))
    fscaling = jnp.sum(jnp.where(fhits, fgates[...], 0.0), axis=0, keepdims=True)
    bscaling = jnp.sum(jnp.where(bhits, bgates[...], 0.0), axis=0, keepdims=True)
    px = onehot(placed(fslots, 0))
    ps = onehot(placed(bslots, MOST))
    ups = placed(bslots, 2 * MOST)
    pu = onehot(ups)
    gate = jnp.sum(jnp.where(ups, bscaling, 0.0), axis=1, keepdims=True)
    hi = fscaling.astype(BF).astype(F32)
    mid = (fscaling - hi).astype(BF).astype(F32)
    low = fscaling - hi - mid
    line = iota((8, TOK), 0)
    rows = jnp.where(line == 0, fslots[:8], bslots[:8])
    for at, value in ((1, hi), (2, mid), (3, low)):
        rows = jnp.where(line == at, value, rows)
    meta[...] = rows

    @pl.loop(0, NODES)
    def _(j):
        for i in range(3):
            fetch(j, i).wait()
        x, saves, raw = (held[i, :, strip(j)] for i in range(3))
        rows = (dot(px, x) + dot(ps, saves) + gate * dot(pu, raw)).astype(BF)
        packed[2 * j] = rows[:, :COLS]
        packed[2 * j + 1] = rows[:, COLS:]


def pick(froutes, fgates, broutes, bgates, acts, saved, cot):
    vmem = pl.BlockSpec(memory_space=pltpu.VMEM)
    anywhere = pl.BlockSpec(memory_space=pl.ANY)
    return pl.pallas_call(
        pick_kernel,
        in_specs=[vmem] * 4 + [anywhere] * 3,
        out_specs=(vmem,) * 2,
        scratch_shapes=[pltpu.VMEM((3, TOK, D), BF), pltpu.SemaphoreType.DMA((NODES, 3))],
        out_shape=(
            jax.ShapeDtypeStruct((2 * NODES, PICK, COLS), BF),
            jax.ShapeDtypeStruct((8, TOK), F32),
        ),
        compiler_params=pltpu.CompilerParams(vmem_limit_bytes=VMEM_MOST),
        name="pick",
    )(froutes, fgates, broutes, bgates, acts, saved, cot)


def spread(rows, places):
    r, c = iota((rows, PICK), 0), iota((rows, PICK), 1)
    out = None
    for start, source in places:
        j = r - start
        here = (j >= 0) & (j < MOST) & (c == j + source)
        out = here if out is None else out | here
    return onehot(out)


def partial_kernel(place, picks, up, down, *refs):
    far, sums = refs[:4], refs[4:6]
    tall, low = 72, 40
    edge = 4 * MOST - 64
    inputs, grads = [], []
    for half in range(2):
        for owner in range(2):
            at = half * tall + owner * MOST
            inputs.append(spread(2 * tall + 8, ((at, MOST), (at + 2 * MOST, 0))))
            grads.append(spread(2 * low, ((half * low + edge + owner * MOST, 2 * MOST),)))

    @pl.loop(0, NODES // 2)
    def _(pair):
        blocks = []
        for half in range(2):
            at = 2 * lax.rem(place[0] + 2 * pair + half, NODES)
            blocks += [picks[at], picks[at + 1]]
        rows = sum(dot(e, block) for e, block in zip(inputs, blocks)).astype(BF)
        ends = sum(dot(e, block) for e, block in zip(grads, blocks)).astype(BF)
        for out, cols in zip(sums, STREAMS):
            ups, downs = dot(rows, up[:, cols]), dot(ends, down[:, cols])
            first = iota((16, cols.stop - cols.start), 0) < edge
            for half in range(2):
                k, i, j = 2 * pair + half, half * tall, half * low
                out[k, :64, :] = ups[i : i + 64].astype(BF)
                mixed = jnp.where(first, ups[i + 64 : i + 80], downs[j : j + 16])
                out[k, 64:80, :] = mixed.astype(BF)
                out[k, 80:, :] = downs[j + 16 : j + low].astype(BF)

    for i, out in enumerate(sums):
        value = out[4]
        far[2 * i][...] = value[:CUT]
        far[2 * i + 1][...] = value[CUT:]


def partial_sums(place, picks, up, down):
    vmem = pl.BlockSpec(memory_space=pltpu.VMEM)
    widths = [cols.stop - cols.start for cols in STREAMS]
    shapes = [jax.ShapeDtypeStruct((rows, w), BF) for w in widths for rows in (CUT, CHUNK - CUT)]
    shapes += [jax.ShapeDtypeStruct((NODES, CHUNK, w), BF) for w in widths]
    return pl.pallas_call(
        partial_kernel,
        out_shape=shapes,
        in_specs=[pl.BlockSpec(memory_space=pltpu.SMEM)] + [vmem] * 3,
        out_specs=[vmem] * len(shapes),
        compiler_params=pltpu.CompilerParams(vmem_limit_bytes=VMEM_LIMIT),
        name="partials",
    )(place, picks, up, down)


def outward_kernel(count, *refs):
    parts, (up, down) = refs[:count], refs[count : count + 2]
    outs, (hold, made) = refs[count + 2 : -2], refs[-2:]
    for i, part in enumerate(parts):
        hold[i] = part[...]

    @pl.loop(0, count)
    def _(i):
        rows = hold[i]
        branch, back = dot_nt(rows[:48], down[...]), dot_nt(rows[32:], up[...])
        made[i, :32, :] = branch[:32].astype(BF)
        line = iota((16, COLS), 0)
        made[i, 32:48, :] = jnp.where(line < 2, branch[32:], back[:16]).astype(BF)
        made[i, 48:, :] = back[16:].astype(BF)

    for i, out in enumerate(outs):
        out[...] = made[i]


def outward(parts, up, down):
    vmem, count = pl.BlockSpec(memory_space=pltpu.VMEM), len(parts)
    return pl.pallas_call(
        functools.partial(outward_kernel, count),
        out_shape=[jax.ShapeDtypeStruct((SENT, COLS), BF)] * count,
        in_specs=[vmem] * (count + 2),
        out_specs=[vmem] * count,
        scratch_shapes=[pltpu.VMEM((count, SENT, FF), BF), pltpu.VMEM((count, SENT, COLS), BF)],
        compiler_params=pltpu.CompilerParams(vmem_limit_bytes=VMEM_LIMIT),
        cost_estimate=pl.CostEstimate(
            flops=4 * count * SENT * COLS * FF, bytes_accessed=4 * COLS * FF, transcendentals=0
        ),
        name="outward",
    )(*parts, up, down)


def settle_kernel(place, meta, *refs):
    parts, outs, held = refs[:NODES], refs[NODES:-1], refs[-1]
    for k, part in enumerate(parts):
        held[k] = part[...]
    r, c = iota((ROWS, SENT), 0), iota((ROWS, SENT), 1)
    line = iota((ROWS, COLS), 0)
    heads = []
    for rows in (((MOST, 0), (MOST + 1, 1), (MOST + 2, 2), (MOST + 3, 3)), ((MOST, 4),)):
        head = jnp.zeros((ROWS, TOK), F32)
        for at, source in rows:
            head = jnp.where(line[:, :TOK] == at, meta[source : source + 1, :], head)
        heads.append(jnp.concatenate([head, jnp.zeros((ROWS, COLS - TOK), F32)], axis=1))
    picks = []
    for start, head in ((0, heads[0]), (2 * MOST, heads[1])):
        for owner in (place[1], 1 - place[1]):
            picks.append((onehot((r < MOST) & (c == r + start + owner * MOST)), head))

    @pl.loop(0, NODES)
    def _(k):
        at = lax.rem(place[0] + k, NODES)
        rows = held[k]
        for (select, head), out in zip(picks, outs):
            out[at] = (dot(select, rows) + head).astype(BF)


def settle(place, meta, parts):
    vmem = pl.BlockSpec(memory_space=pltpu.VMEM)
    return pl.pallas_call(
        settle_kernel,
        out_shape=(jax.ShapeDtypeStruct((NODES, ROWS, COLS), BF),) * 4,
        in_specs=[pl.BlockSpec(memory_space=pltpu.SMEM)] + [vmem] * (NODES + 1),
        out_specs=(vmem,) * 4,
        scratch_shapes=[pltpu.VMEM((NODES, SENT, COLS), BF)],
        compiler_params=pltpu.CompilerParams(vmem_limit_bytes=VMEM_LIMIT),
        name="settle",
    )(place, meta, *parts)


def patch_kernel(place, fraw, fown, fother, braw, bown, bother, fout, bout):
    first = place[1] == 0
    line = iota((ROWS, TOK), 0)
    ones = jnp.ones((ROWS, TOK), BF)
    for raw, own, other, out, scaled in (
        (fraw, fown, fother, fout, True),
        (braw, bown, bother, bout, False),
    ):
        head = own[0, :, :TOK]
        slots = jnp.sum(jnp.where(line == MOST, head.astype(F32), 0.0), axis=0, keepdims=True)
        chosen = onehot((slots == line.astype(F32)) & (line < MOST))
        if scaled:
            three = jnp.where((line > MOST) & (line < MOST + 4), head.astype(F32), 0.0).astype(BF)
            scaling = jnp.concatenate([dot_tn(three, ones)] * (WIDE // TOK), axis=1)
        for j in range(own.shape[0]):
            mine, theirs = own[j], other[j]
            rows = jnp.concatenate(
                [jnp.where(first, mine, theirs), jnp.where(first, theirs, mine)], axis=1
            )
            fresh = dot_tn(chosen, rows)
            if scaled:
                fresh = scaling * fresh
            cols = slice(j * WIDE, (j + 1) * WIDE)
            out[:, cols] = (raw[:, cols].astype(F32) + fresh).astype(BF)


def patch(place, fraw, fown, fother, braw, bown, bother):
    steps = 4
    strip = pl.BlockSpec((TOK, D // steps), lambda i: (0, i))
    rows = pl.BlockSpec((NODES // steps, ROWS, COLS), lambda i: (i, 0, 0))
    return pl.pallas_call(
        patch_kernel,
        grid=(steps,),
        out_shape=(jax.ShapeDtypeStruct((TOK, D), BF),) * 2,
        in_specs=[pl.BlockSpec(memory_space=pltpu.SMEM), strip, rows, rows, strip, rows, rows],
        out_specs=(strip, strip),
        compiler_params=pltpu.CompilerParams(vmem_limit_bytes=VMEM_LIMIT),
        name="patch",
    )(place, fraw, fown, fother, braw, bown, bother)


def around(value, steps):
    pairs = [(2 * z + x, 2 * ((z + steps) % NODES) + x) for z in range(NODES) for x in range(2)]
    return lax.ppermute(value, "expert", pairs)


def across_x(value):
    return lax.ppermute(value, "expert", [(e, e ^ 1) for e in range(2 * NODES)])


def section_shift(value, steps, flip=0):
    sections, experts = lax.axis_size("section"), lax.axis_size("expert")
    pairs = [
        (s * experts + e, (s + steps) % sections * experts + (e ^ flip))
        for s in range(sections)
        for e in range(experts)
    ]
    return lax.ppermute(value, ("section", "expert"), pairs)


def add(*terms):
    return functools.reduce(lambda a, b: a + b, [t.astype(F32) for t in terms]).astype(BF)


def scatter_ring(right, left, part):
    right, left = around(right, 1), around(left, -1)
    right = jnp.concatenate([add(part[3, :CUT], right), part[3, CUT:]])
    left = jnp.concatenate([part[5, :CUT], add(part[5, CUT:], left)])
    for k in (2, 1):
        right = add(part[k], around(right, 1))
        left = add(part[NODES - k], around(left, -1))
    total = add(part[0], around(right, 1), around(left, -1))
    return total.astype(F32) + across_x(total).astype(F32)


def activate(total):
    before = total[: 2 * MOST]
    hidden = jax.nn.silu(total[2 * MOST : 4 * MOST])
    grad = total[4 * MOST : 6 * MOST]
    sigma = jax.nn.sigmoid(before)
    pre_grad = grad * (sigma * (1.0 + before * (1.0 - sigma)))
    pad = jnp.zeros((SENT - 4 * MOST, total.shape[1]), F32)
    return jnp.concatenate([hidden, pre_grad, pad]).astype(BF)


def gather_ring(mine, up, down):
    half = 32
    back = [None] * NODES
    right, left = around(mine, 1), around(mine, -1)
    made = outward([mine], up, down)
    right, left, back[0] = lax.optimization_barrier((right, left, made[0]))
    for k in (1, 2, 3):
        if k < 3:
            onward = around(right, 1), around(left, -1)
        else:
            onward = around(right[:half], 1), around(left[half:], -1)
        one, two = outward([right, left], up, down)
        back[k], back[NODES - k] = around(one, -k), around(two, k)
        if k > 1:
            onward, one, two, back[k - 1], back[NODES - k + 1] = lax.optimization_barrier(
                (onward, one, two, back[k - 1], back[NODES - k + 1])
            )
        else:
            onward, one, two = lax.optimization_barrier((onward, one, two))
        right, left = onward
    (far,) = outward([jnp.concatenate([right, left])], up, down)
    back[4] = around(far, 4)
    return back


def per_device(
    forward_in,
    backward_saved,
    backward_grad,
    forward_routes,
    forward_gates,
    backward_routes,
    backward_gates,
    up_weight,
    down_weight,
):
    up, down = up_weight[0], down_weight[0].T
    expert = lax.axis_index("expert").astype(jnp.int32)
    place = jnp.stack([expert // 2, expert % 2])
    packed, meta = pick(
        forward_routes[0].T,
        forward_gates[0].T,
        backward_routes[0].T,
        backward_gates[0].T,
        forward_in[0],
        backward_saved[0],
        backward_grad[0],
    )
    packed, acts, cot = lax.optimization_barrier((packed, forward_in[0], backward_grad[0]))
    picks = lax.all_to_all(packed, "expert", split_axis=0, concat_axis=0, tiled=True)
    fraw, braw = section_shift(acts, 1), section_shift(cot, -1)
    (right1, left1, right2, left2, part1, part2), fraw, braw = lax.optimization_barrier(
        (partial_sums(place, picks, up, down), fraw, braw)
    )
    totals = [scatter_ring(right1, left1, part1), scatter_ring(right2, left2, part2)]
    mine = jnp.concatenate([activate(total) for total in totals], axis=1)
    back = gather_ring(mine, up, down)
    fown, fother, bown, bother = settle(place, meta, back)
    forward_out, backward_out = patch(
        place,
        fraw,
        section_shift(fown, 1),
        section_shift(fother, 1, 1),
        braw,
        section_shift(bown, -1),
        section_shift(bother, -1, 1),
    )
    return forward_out[None], backward_out[None]


def solution(mesh):
    row = P("section", "expert", None)
    return jax.shard_map(
        per_device,
        mesh=mesh,
        in_specs=(row, row, row, row, row, row, row, row, P("section", None, "expert")),
        out_specs=(row, row),
        check_vma=False,
    )
```

profile of v0, /device:TPU:1, one launch (start us, length us, event | category | flops | bytes accessed | tf_op | source)
XLA Modules:
  0.0 188.3 jit_solution(7920923076976041812)
XLA Ops:
  0.6 5.7 %pick.1 = (bf16[16,56,448]{2,1,0:T(8,128)(2,1)}, f32[8,128]{1,0:T(8,128)}) custom-call(s32[2,128]{1,0:T(2,128)} %bitcast.86, f32[2,128]{1,0:T(2,128)} %bitcast.87, s32[2,128]{1,0:T(2,128)} %bitcast.88, f32[2,128]{1,0:T(2,128)} %bitcast.89, bf16[128,7168]{1,0:T(8,128)(2,1)} %bitcast.10.acts, bf16[128,7168]{1,0:T(8,128)(2,1)} %bitcast.85, ...), custom_call_target="tpu_custom_call" | custom-call | tf_op jit(solution)/shard_map/pick/pallas_call | solution.py:109
  6.4 2.8 %collective-permute-start = (bf16[128,7168]{1,0:T(8,128)(2,1)}, bf16[128,7168]{1,0:T(8,128)(2,1)S(1)}, u32[]{:S(2)}, u32[]{:S(2)}) collective-permute-start(bf16[128,7168]{1,0:T(8,128)(2,1)} %bitcast.10.acts), channel_id=1, source_target_pairs={{0,16},{1,17},{2,18},{3,19},{4,20},{5,21},{6,22},{7,23},{8,24},{9,... | collective-permute-start | bytes 5505032 | tf_op jit(solution)/shard_map/ppermute | solution.py:313
  9.8 8.6 %all-to-all-start = ((bf16[16,56,448]{2,1,0:T(8,128)(2,1)}), bf16[16,56,448]{2,1,0:T(8,128)(2,1)S(1)}, u32[]{:S(2)}, u32[]{:S(2)}) async-start(bf16[16,56,448]{2,1,0:T(8,128)(2,1)} %get-tuple-element.47), calls=%async_computation | async-start | bytes 1835008 | tf_op jit(solution)/shard_map/all_to_all | solution.py:390
  18.5 19.1 %all-to-all-done.picks = bf16[16,56,448]{2,1,0:T(8,128)(2,1)S(1)} async-done(((bf16[16,56,448]{2,1,0:T(8,128)(2,1)}), bf16[16,56,448]{2,1,0:T(8,128)(2,1)S(1)}, u32[]{:S(2)}, u32[]{:S(2)}) %all-to-all-start) | async-done | bytes 802848 | tf_op jit(solution)/shard_map/all_to_all | solution.py:390
  37.6 6.8 %partials.1 = (bf16[48,1280]{1,0:T(8,128)(2,1)S(1)}, bf16[56,1280]{1,0:T(8,128)(2,1)S(1)}, bf16[48,1152]{1,0:T(8,128)(2,1)S(1)}, bf16[56,1152]{1,0:T(8,128)(2,1)...) custom-call(s32[2]{0:T(128)S(1)} %pad_add_fusion.place, ...), custom_call_target="tpu_custom_call" | custom-call | tf_op jit(solution)/shard_map/partials/pallas_call | solution.py:173
  44.7 2.7 %collective-permute-start.15 = (bf16[56,1152]{1,0:T(8,128)(2,1)S(1)}, bf16[56,1152]{1,0:T(8,128)(2,1)S(1)}, u32[]{:S(2)}, u32[]{:S(2)}) collective-permute-start(bf16[56,1152]{1,0:T(8,128)(2,1)S(1)} %get-tuple-element.63), channel_id=1, source_target_pairs={{0,14},{1,15},{2,0},{3,1},{4,2},{5,3},{6,4},{7,5},{8,6},{9,7},{10,... | collective-permute-start | bytes 387080 | tf_op jit(solution)/shard_map/ppermute | solution.py:299
  47.3 2.7 %collective-permute-start.6 = (bf16[56,1280]{1,0:T(8,128)(2,1)S(1)}, bf16[56,1280]{1,0:T(8,128)(2,1)S(1)}, u32[]{:S(2)}, u32[]{:S(2)}) collective-permute-start(bf16[56,1280]{1,0:T(8,128)(2,1)S(1)} %get-tuple-element.60), channel_id=1, source_target_pairs={{0,14},{1,15},{2,0},{3,1},{4,2},{5,3},{6,4},{7,5},{8,6},{9,7},{10,... | collective-permute-start | bytes 430088 | tf_op jit(solution)/shard_map/ppermute | solution.py:299
  50.2 2.1 %collective-permute-done.2 = bf16[48,1280]{1,0:T(8,128)(2,1)S(1)} collective-permute-done((bf16[48,1280]{1,0:T(8,128)(2,1)S(1)}, bf16[48,1280]{1,0:T(8,128)(2,1)S(1)}, u32[]{:S(2)}, u32[]{:S(2)}) %collective-permute-start.2) | collective-permute-done | bytes 122912 | tf_op jit(solution)/shard_map/ppermute | solution.py:299
  52.5 2.7 %collective-permute-start.16 = (bf16[104,1152]{1,0:T(8,128)(2,1)S(1)}, bf16[104,1152]{1,0:T(8,128)(2,1)S(1)}, u32[]{:S(2)}, u32[]{:S(2)}) collective-permute-start(bf16[104,1152]{1,0:T(8,128)(2,1)S(1)} %pad_maximum_fusion.4), channel_id=1, source_target_pairs={{0,14},{1,15},{2,0},{3,1},{4,2},{5,3},{6,4},{7,5},{8,6},{9,7},{10,... | collective-permute-start | bytes 718856 | tf_op jit(solution)/shard_map/ppermute | solution.py:299
  55.4 0.9 collective-permute-done.12
  57.0 2.2 %collective-permute-done.3 = bf16[104,1280]{1,0:T(8,128)(2,1)S(1)} collective-permute-done((bf16[104,1280]{1,0:T(8,128)(2,1)S(1)}, bf16[104,1280]{1,0:T(8,128)(2,1)S(1)}, u32[]{:S(2)}, u32[]{:S(2)}) %collective-permute-start.3) | collective-permute-done | bytes 266272 | tf_op jit(solution)/shard_map/ppermute | solution.py:299
  59.4 4.7 %collective-permute-done.13 = bf16[104,1152]{1,0:T(8,128)(2,1)S(1)} collective-permute-done((bf16[104,1152]{1,0:T(8,128)(2,1)S(1)}, bf16[104,1152]{1,0:T(8,128)(2,1)S(1)}, u32[]{:S(2)}, u32[]{:S(2)}) %collective-permute-start.13) | collective-permute-done | bytes 239648 | tf_op jit(solution)/shard_map/ppermute | solution.py:299
  64.4 1.5 collective-permute-start.14
  65.8 3.0 %collective-permute-done.4 = bf16[104,1280]{1,0:T(8,128)(2,1)S(1)} collective-permute-done((bf16[104,1280]{1,0:T(8,128)(2,1)S(1)}, bf16[104,1280]{1,0:T(8,128)(2,1)S(1)}, u32[]{:S(2)}, u32[]{:S(2)}) %collective-permute-start.4) | collective-permute-done | bytes 266272 | tf_op jit(solution)/shard_map/ppermute | solution.py:299
  69.0 1.5 collective-permute-start.5
  70.5 1.4 collective-permute-start.18
  71.9 5.5 %collective-permute-done.8 = bf16[104,1280]{1,0:T(8,128)(2,1)S(1)} collective-permute-done((bf16[104,1280]{1,0:T(8,128)(2,1)S(1)}, bf16[104,1280]{1,0:T(8,128)(2,1)S(1)}, u32[]{:S(2)}, u32[]{:S(2)}) %collective-permute-start.8) | collective-permute-done | bytes 266272 | tf_op jit(solution)/shard_map/ppermute | solution.py:299
  77.6 3.2 %collective-permute-done.18 = bf16[104,1152]{1,0:T(8,128)(2,1)S(1)} collective-permute-done((bf16[104,1152]{1,0:T(8,128)(2,1)S(1)}, bf16[104,1152]{1,0:T(8,128)(2,1)S(1)}, u32[]{:S(2)}, u32[]{:S(2)}) %collective-permute-start.18) | collective-permute-done | bytes 239648 | tf_op jit(solution)/shard_map/ppermute | solution.py:299
  81.3 2.4 %collective-permute-done.9 = bf16[104,1280]{1,0:T(8,128)(2,1)S(1)} collective-permute-done((bf16[104,1280]{1,0:T(8,128)(2,1)S(1)}, bf16[104,1280]{1,0:T(8,128)(2,1)S(1)}, u32[]{:S(2)}, u32[]{:S(2)}) %collective-permute-start.9) | collective-permute-done | bytes 266272 | tf_op jit(solution)/shard_map/ppermute | solution.py:299
  84.1 2.1 %collective-permute-done.19 = bf16[104,1152]{1,0:T(8,128)(2,1)S(1)} collective-permute-done((bf16[104,1152]{1,0:T(8,128)(2,1)S(1)}, bf16[104,1152]{1,0:T(8,128)(2,1)S(1)}, u32[]{:S(2)}, u32[]{:S(2)}) %collective-permute-start.19) | collective-permute-done | bytes 239648 | tf_op jit(solution)/shard_map/ppermute | solution.py:303
  86.5 2.7 %collective-permute-done.10 = bf16[104,1280]{1,0:T(8,128)(2,1)S(1)} collective-permute-done((bf16[104,1280]{1,0:T(8,128)(2,1)S(1)}, bf16[104,1280]{1,0:T(8,128)(2,1)S(1)}, u32[]{:S(2)}, u32[]{:S(2)}) %collective-permute-start.10) | collective-permute-done | bytes 266272 | tf_op jit(solution)/shard_map/ppermute | solution.py:303
  90.4 2.7 %collective-permute-start.21 = (bf16[72,2432]{1,0:T(8,128)(2,1)S(1)}, bf16[72,2432]{1,0:T(8,128)(2,1)S(1)}, u32[]{:S(2)}, u32[]{:S(2)}) collective-permute-start(bf16[72,2432]{1,0:T(8,128)(2,1)S(1)} %maximum_maximum_fusion.refs_0_), channel_id=1, source_target_pairs={{0,14},{1,15},{2,0},{3,1},{4,2},{5,3},{6,4},{7,5},{8,6},{9,7},{10,... | collective-permute-start | bytes 1050632 | tf_op jit(solution)/shard_map/ppermute | solution.py:299
  93.1 1.3 outward.5.refs_0_
  94.5 3.3 %collective-permute-done.20.refs_0_ = bf16[72,2432]{1,0:T(8,128)(2,1)S(1)} collective-permute-done((bf16[72,2432]{1,0:T(8,128)(2,1)S(1)}, bf16[72,2432]{1,0:T(8,128)(2,1)S(1)}, u32[]{:S(2)}, u32[]{:S(2)}) %collective-permute-start.20) | collective-permute-done | bytes 350240 | tf_op jit(solution)/shard_map/ppermute | solution.py:299
  97.7 3.4 %collective-permute-done.21.refs_1_ = bf16[72,2432]{1,0:T(8,128)(2,1)S(1)} collective-permute-done((bf16[72,2432]{1,0:T(8,128)(2,1)S(1)}, bf16[72,2432]{1,0:T(8,128)(2,1)S(1)}, u32[]{:S(2)}, u32[]{:S(2)}) %collective-permute-start.21) | collective-permute-done | bytes 350240 | tf_op jit(solution)/shard_map/ppermute | solution.py:299
  101.7 2.2 %collective-permute-start.23 = (bf16[72,2432]{1,0:T(8,128)(2,1)S(1)}, bf16[72,2432]{1,0:T(8,128)(2,1)S(1)}, u32[]{:S(2)}, u32[]{:S(2)}) collective-permute-start(bf16[72,2432]{1,0:T(8,128)(2,1)S(1)} %collective-permute-done.21.refs_1_), channel_id=1, source_target_pairs={{0,14},{1,15},{2,0},{3,1},{4,2},{5,3},{6,4},{7,5},{8,6},{9,7},{10,... | collective-permute-start | bytes 1050632 | tf_op jit(solution)/shard_map/ppermute | solution.py:299
  103.8 2.7 %outward.6 = (bf16[72,448]{1,0:T(8,128)(2,1)S(1)}, bf16[72,448]{1,0:T(8,128)(2,1)S(1)}) custom-call(bf16[72,2432]{1,0:T(8,128)(2,1)S(1)} %collective-permute-done.20.refs_0_, bf16[72,2432]{1,0:T(8,128)(2,1)S(1)} %collective-permute-done.21.refs_1_, bf16[448,2432]{1,0:T(8,128)(2,1)S(1)} %bitcast.75, bf16[448,2432]{1,0:T(8,128)(2,1)S(1)} %bitcast.81), custom_call_target="tpu_custom_call" | custom-call | flops 627572736 | bytes 4358144 | tf_op jit(solution)/shard_map/outward/pallas_call | solution.py:204
  106.5 2.0 %collective-permute-done.22.refs_0_ = bf16[72,2432]{1,0:T(8,128)(2,1)S(1)} collective-permute-done((bf16[72,2432]{1,0:T(8,128)(2,1)S(1)}, bf16[72,2432]{1,0:T(8,128)(2,1)S(1)}, u32[]{:S(2)}, u32[]{:S(2)}) %collective-permute-start.22) | collective-permute-done | bytes 350240 | tf_op jit(solution)/shard_map/ppermute | solution.py:299
  108.6 1.0 collective-permute-start.24
  109.5 1.7 collective-permute-start.25
  111.2 1.5 collective-permute-start.26
  112.7 2.7 %outward.7 = (bf16[72,448]{1,0:T(8,128)(2,1)S(1)}, bf16[72,448]{1,0:T(8,128)(2,1)S(1)}) custom-call(bf16[72,2432]{1,0:T(8,128)(2,1)S(1)} %collective-permute-done.22.refs_0_, bf16[72,2432]{1,0:T(8,128)(2,1)S(1)} %collective-permute-done.23.refs_1_, bf16[448,2432]{1,0:T(8,128)(2,1)S(1)} %bitcast.76, bf16[448,2432]{1,0:T(8,128)(2,1)S(1)} %bitcast.82), custom_call_target="tpu_custom_call" | custom-call | flops 627572736 | bytes 4358144 | tf_op jit(solution)/shard_map/outward/pallas_call | solution.py:204
  115.4 5.1 %collective-permute-done.26.refs_1_ = bf16[72,448]{1,0:T(8,128)(2,1)S(1)} collective-permute-done((bf16[72,448]{1,0:T(8,128)(2,1)S(1)}, bf16[72,448]{1,0:T(8,128)(2,1)S(1)}, u32[]{:S(2)}, u32[]{:S(2)}) %collective-permute-start.26) | collective-permute-done | bytes 64544 | tf_op jit(solution)/shard_map/ppermute | solution.py:299
  120.7 2.4 %collective-permute-start.29 = (bf16[40,2432]{1,0:T(8,128)(2,1)S(1)}, bf16[40,2432]{1,0:T(8,128)(2,1)S(1)}, u32[]{:S(2)}, u32[]{:S(2)}) collective-permute-start(bf16[40,2432]{1,0:T(8,128)(2,1)S(1)} %slice.103), channel_id=1, source_target_pairs={{0,14},{1,15},{2,0},{3,1},{4,2},{5,3},{6,4},{7,5},{8,6},{9,7},{10,... | collective-permute-start | bytes 583688 | tf_op jit(solution)/shard_map/ppermute | solution.py:299
  123.3 1.5 collective-permute-start.30
  125.7 2.7 %outward.8 = (bf16[72,448]{1,0:T(8,128)(2,1)S(1)}, bf16[72,448]{1,0:T(8,128)(2,1)S(1)}) custom-call(bf16[72,2432]{1,0:T(8,128)(2,1)S(1)} %collective-permute-done.24.refs_0_, bf16[72,2432]{1,0:T(8,128)(2,1)S(1)} %collective-permute-done.25.refs_1_, bf16[448,2432]{1,0:T(8,128)(2,1)S(1)} %bitcast.77, bf16[448,2432]{1,0:T(8,128)(2,1)S(1)} %bitcast.83), custom_call_target="tpu_custom_call" | custom-call | flops 627572736 | bytes 4358144 | tf_op jit(solution)/shard_map/outward/pallas_call | solution.py:204
  128.4 2.4 %collective-permute-start.32 = (bf16[72,448]{1,0:T(8,128)(2,1)S(1)}, bf16[72,448]{1,0:T(8,128)(2,1)S(1)}, u32[]{:S(2)}, u32[]{:S(2)}) collective-permute-start(bf16[72,448]{1,0:T(8,128)(2,1)S(1)} %get-tuple-element.76), channel_id=1, source_target_pairs={{0,10},{1,11},{2,12},{3,13},{4,14},{5,15},{6,0},{7,1},{8,2},{9,3},... | collective-permute-start | bytes 193544 | tf_op jit(solution)/shard_map/ppermute | solution.py:299
  130.8 1.0 collective-permute-start.34
  131.8 1.3 outward.9
  133.1 3.9 %collective-permute-start.33 = (bf16[72,448]{1,0:T(8,128)(2,1)S(1)}, bf16[72,448]{1,0:T(8,128)(2,1)S(1)}, u32[]{:S(2)}, u32[]{:S(2)}) collective-permute-start(bf16[72,448]{1,0:T(8,128)(2,1)S(1)} %outward.9), channel_id=1, source_target_pairs={{0,8},{1,9},{2,10},{3,11},{4,12},{5,13},{6,14},{7,15},{8,0},{9,1},... | collective-permute-start | bytes 193544 | tf_op jit(solution)/shard_map/ppermute | solution.py:299
  137.0 1.2 collective-permute-done.34.refs_5_
  138.3 4.0 %collective-permute-done.33.refs_4_ = bf16[72,448]{1,0:T(8,128)(2,1)S(1)} collective-permute-done((bf16[72,448]{1,0:T(8,128)(2,1)S(1)}, bf16[72,448]{1,0:T(8,128)(2,1)S(1)}, u32[]{:S(2)}, u32[]{:S(2)}) %collective-permute-start.33) | collective-permute-done | bytes 64544 | tf_op jit(solution)/shard_map/ppermute | solution.py:299
  142.2 2.0 %settle.1 = (bf16[8,24,448]{2,1,0:T(8,128)(2,1)S(1)}, bf16[8,24,448]{2,1,0:T(8,128)(2,1)S(1)}, bf16[8,24,448]{2,1,0:T(8,128)(2,1)S(1)}, bf16[8,24,448]{2,1,0:T(8,128)(2,1)S(1)}) custom-call(s32[2]{0:T(128)S(1)} %pad_add_fusion.place, f32[8,128]{1,0:T(8,128)S(1)} %copy-done.2, bf16[72,448]{1,0:T(8,128)(2,1)S(1)} %outward.5.refs_0_, ...), custom_call_target="tpu_custom_call" | custom-call | tf_op jit(solution)/shard_map/settle/pallas_call | solution.py:245
  144.2 27.4 %collective-permute-start.35 = (bf16[8,24,448]{2,1,0:T(8,128)(2,1)S(1)}, bf16[8,24,448]{2,1,0:T(8,128)(2,1)S(1)}, u32[]{:S(2)}, u32[]{:S(2)}) collective-permute-start(bf16[8,24,448]{2,1,0:T(8,128)(2,1)S(1)} %get-tuple-element.83), channel_id=1, source_target_pairs={{0,16},{1,17},{2,18},{3,19},{4,20},{5,21},{6,22},{7,23},{8,24},{9,... | collective-permute-start | bytes 516104 | tf_op jit(solution)/shard_map/ppermute | solution.py:313
  171.8 4.8 %collective-permute-start.38 = (bf16[8,24,448]{2,1,0:T(8,128)(2,1)S(1)}, bf16[8,24,448]{2,1,0:T(8,128)(2,1)S(1)}, u32[]{:S(2)}, u32[]{:S(2)}) collective-permute-start(bf16[8,24,448]{2,1,0:T(8,128)(2,1)S(1)} %get-tuple-element.87), channel_id=1, source_target_pairs={{0,241},{1,240},{2,243},{3,242},{4,245},{5,244},{6,247},{7,246},{8... | collective-permute-start | bytes 516104 | tf_op jit(solution)/shard_map/ppermute | solution.py:313
  176.6 1.7 collective-permute-done.36.fother
  178.3 5.3 %collective-permute-done.38.bother = bf16[8,24,448]{2,1,0:T(8,128)(2,1)S(1)} collective-permute-done((bf16[8,24,448]{2,1,0:T(8,128)(2,1)S(1)}, bf16[8,24,448]{2,1,0:T(8,128)(2,1)S(1)}, u32[]{:S(2)}, u32[]{:S(2)}) %collective-permute-start.38) | collective-permute-done | bytes 172064 | tf_op jit(solution)/shard_map/ppermute | solution.py:313
  183.7 4.6 %patch.1 = (bf16[128,7168]{1,0:T(8,128)(2,1)}, bf16[128,7168]{1,0:T(8,128)(2,1)}) custom-call(s32[2]{0:T(128)S(1)} %pad_add_fusion.place, bf16[128,7168]{1,0:T(8,128)(2,1)S(1)} %collective-permute-done.fraw, bf16[8,24,448]{2,1,0:T(8,128)(2,1)S(1)} %collective-permute-done.35.fown, bf16[8,24,448]{2,1,0:T(8,128)(2,1)S(1)} %collective-permute-done.36.fother, ...), custom_call_target="tpu_custom_call" | custom-call | tf_op jit(solution)/shard_map/patch/pallas_call | solution.py:286
  (78 shorter events, 7.2 us)
Async XLA Ops:
  6.4 38.0 %collective-permute-start = (bf16[128,7168]{1,0:T(8,128)(2,1)}, bf16[128,7168]{1,0:T(8,128)(2,1)S(1)}, u32[]{:S(2)}, u32[]{:S(2)}) collective-permute-start(bf16[128,7168]{1,0:T(8,128)(2,1)} %bitcast.10.acts), channel_id=1, source_target_pairs={{0,16},{1,17},{2,18},{3,19},{4,20},{5,21},{6,22},{7,23},{8,24},{9,... | collective-permute-start | bytes 5505032 | tf_op jit(solution)/shard_map/ppermute | solution.py:313
  9.1 35.3 %collective-permute-start.1 = (bf16[128,7168]{1,0:T(8,128)(2,1)}, bf16[128,7168]{1,0:T(8,128)(2,1)}, u32[]{:S(2)}, u32[]{:S(2)}) collective-permute-start(bf16[128,7168]{1,0:T(8,128)(2,1)} %bitcast.12.cot), channel_id=1, source_target_pairs={{0,240},{1,241},{2,242},{3,243},{4,244},{5,245},{6,246},{7,247},{8... | collective-permute-start | bytes 5505032 | tf_op jit(solution)/shard_map/ppermute | solution.py:313
  9.8 27.8 %all-to-all-start = ((bf16[16,56,448]{2,1,0:T(8,128)(2,1)}), bf16[16,56,448]{2,1,0:T(8,128)(2,1)S(1)}, u32[]{:S(2)}, u32[]{:S(2)}) async-start(bf16[16,56,448]{2,1,0:T(8,128)(2,1)} %get-tuple-element.47), calls=%async_computation | async-start | bytes 1835008 | tf_op jit(solution)/shard_map/all_to_all | solution.py:390
  44.5 5.5 %collective-permute-start.11 = (bf16[48,1152]{1,0:T(8,128)(2,1)S(1)}, bf16[48,1152]{1,0:T(8,128)(2,1)S(1)}, u32[]{:S(2)}, u32[]{:S(2)}) collective-permute-start(bf16[48,1152]{1,0:T(8,128)(2,1)S(1)} %get-tuple-element.62), channel_id=1, source_target_pairs={{0,2},{1,3},{2,4},{3,5},{4,6},{5,7},{6,8},{7,9},{8,10},{9,11},{10,... | collective-permute-start | bytes 331784 | tf_op jit(solution)/shard_map/ppermute | solution.py:299
  44.7 7.8 %collective-permute-start.15 = (bf16[56,1152]{1,0:T(8,128)(2,1)S(1)}, bf16[56,1152]{1,0:T(8,128)(2,1)S(1)}, u32[]{:S(2)}, u32[]{:S(2)}) collective-permute-start(bf16[56,1152]{1,0:T(8,128)(2,1)S(1)} %get-tuple-element.63), channel_id=1, source_target_pairs={{0,14},{1,15},{2,0},{3,1},{4,2},{5,3},{6,4},{7,5},{8,6},{9,7},{10,... | collective-permute-start | bytes 387080 | tf_op jit(solution)/shard_map/ppermute | solution.py:299
  47.3 4.9 %collective-permute-start.2 = (bf16[48,1280]{1,0:T(8,128)(2,1)S(1)}, bf16[48,1280]{1,0:T(8,128)(2,1)S(1)}, u32[]{:S(2)}, u32[]{:S(2)}) collective-permute-start(bf16[48,1280]{1,0:T(8,128)(2,1)S(1)} %get-tuple-element.59), channel_id=1, source_target_pairs={{0,2},{1,3},{2,4},{3,5},{4,6},{5,7},{6,8},{7,9},{8,10},{9,11},{10,... | collective-permute-start | bytes 368648 | tf_op jit(solution)/shard_map/ppermute | solution.py:299
  47.3 7.9 %collective-permute-start.6 = (bf16[56,1280]{1,0:T(8,128)(2,1)S(1)}, bf16[56,1280]{1,0:T(8,128)(2,1)S(1)}, u32[]{:S(2)}, u32[]{:S(2)}) collective-permute-start(bf16[56,1280]{1,0:T(8,128)(2,1)S(1)} %get-tuple-element.60), channel_id=1, source_target_pairs={{0,14},{1,15},{2,0},{3,1},{4,2},{5,3},{6,4},{7,5},{8,6},{9,7},{10,... | collective-permute-start | bytes 430088 | tf_op jit(solution)/shard_map/ppermute | solution.py:299
  50.1 6.3 %collective-permute-start.12 = (bf16[104,1152]{1,0:T(8,128)(2,1)S(1)}, bf16[104,1152]{1,0:T(8,128)(2,1)S(1)}, u32[]{:S(2)}, u32[]{:S(2)}) collective-permute-start(bf16[104,1152]{1,0:T(8,128)(2,1)S(1)} %pad_maximum_fusion.3), channel_id=1, source_target_pairs={{0,2},{1,3},{2,4},{3,5},{4,6},{5,7},{6,8},{7,9},{8,10},{9,11},{10,... | collective-permute-start | bytes 718856 | tf_op jit(solution)/shard_map/ppermute | solution.py:299
  52.3 6.9 %collective-permute-start.3 = (bf16[104,1280]{1,0:T(8,128)(2,1)S(1)}, bf16[104,1280]{1,0:T(8,128)(2,1)S(1)}, u32[]{:S(2)}, u32[]{:S(2)}) collective-permute-start(bf16[104,1280]{1,0:T(8,128)(2,1)S(1)} %pad_maximum_fusion.1), channel_id=1, source_target_pairs={{0,2},{1,3},{2,4},{3,5},{4,6},{5,7},{6,8},{7,9},{8,10},{9,11},{10,... | collective-permute-start | bytes 798728 | tf_op jit(solution)/shard_map/ppermute | solution.py:299
  52.5 6.9 %collective-permute-start.16 = (bf16[104,1152]{1,0:T(8,128)(2,1)S(1)}, bf16[104,1152]{1,0:T(8,128)(2,1)S(1)}, u32[]{:S(2)}, u32[]{:S(2)}) collective-permute-start(bf16[104,1152]{1,0:T(8,128)(2,1)S(1)} %pad_maximum_fusion.4), channel_id=1, source_target_pairs={{0,14},{1,15},{2,0},{3,1},{4,2},{5,3},{6,4},{7,5},{8,6},{9,7},{10,... | collective-permute-start | bytes 718856 | tf_op jit(solution)/shard_map/ppermute | solution.py:299
  55.3 10.5 %collective-permute-start.7 = (bf16[104,1280]{1,0:T(8,128)(2,1)S(1)}, bf16[104,1280]{1,0:T(8,128)(2,1)S(1)}, u32[]{:S(2)}, u32[]{:S(2)}) collective-permute-start(bf16[104,1280]{1,0:T(8,128)(2,1)S(1)} %pad_maximum_fusion.2), channel_id=1, source_target_pairs={{0,14},{1,15},{2,0},{3,1},{4,2},{5,3},{6,4},{7,5},{8,6},{9,7},{10,... | collective-permute-start | bytes 798728 | tf_op jit(solution)/shard_map/ppermute | solution.py:299
  56.4 7.7 %collective-permute-start.13 = (bf16[104,1152]{1,0:T(8,128)(2,1)S(1)}, bf16[104,1152]{1,0:T(8,128)(2,1)S(1)}, u32[]{:S(2)}, u32[]{:S(2)}) collective-permute-start(bf16[104,1152]{1,0:T(8,128)(2,1)S(1)} %fusion.8), channel_id=1, source_target_pairs={{0,2},{1,3},{2,4},{3,5},{4,6},{5,7},{6,8},{7,9},{8,10},{9,11},{10,... | collective-permute-start | bytes 718856 | tf_op jit(solution)/shard_map/ppermute | solution.py:299
  59.3 9.5 %collective-permute-start.4 = (bf16[104,1280]{1,0:T(8,128)(2,1)S(1)}, bf16[104,1280]{1,0:T(8,128)(2,1)S(1)}, u32[]{:S(2)}, u32[]{:S(2)}) collective-permute-start(bf16[104,1280]{1,0:T(8,128)(2,1)S(1)} %fusion.2), channel_id=1, source_target_pairs={{0,2},{1,3},{2,4},{3,5},{4,6},{5,7},{6,8},{7,9},{8,10},{9,11},{10,... | collective-permute-start | bytes 798728 | tf_op jit(solution)/shard_map/ppermute | solution.py:299
  64.3 6.2 %collective-permute-start.17 = (bf16[104,1152]{1,0:T(8,128)(2,1)S(1)}, bf16[104,1152]{1,0:T(8,128)(2,1)S(1)}, u32[]{:S(2)}, u32[]{:S(2)}) collective-permute-start(bf16[104,1152]{1,0:T(8,128)(2,1)S(1)} %get-tuple-element.93), channel_id=1, source_target_pairs={{0,14},{1,15},{2,0},{3,1},{4,2},{5,3},{6,4},{7,5},{8,6},{9,7},{10,... | collective-permute-start | bytes 718856 | tf_op jit(solution)/shard_map/ppermute | solution.py:299
  64.4 13.2 %collective-permute-start.14 = (bf16[104,1152]{1,0:T(8,128)(2,1)S(1)}, bf16[104,1152]{1,0:T(8,128)(2,1)S(1)}, u32[]{:S(2)}, u32[]{:S(2)}) collective-permute-start(bf16[104,1152]{1,0:T(8,128)(2,1)S(1)} %get-tuple-element.92), channel_id=1, source_target_pairs={{0,2},{1,3},{2,4},{3,5},{4,6},{5,7},{6,8},{7,9},{8,10},{9,11},{10,... | collective-permute-start | bytes 718856 | tf_op jit(solution)/shard_map/ppermute | solution.py:299
  68.9 8.5 %collective-permute-start.8 = (bf16[104,1280]{1,0:T(8,128)(2,1)S(1)}, bf16[104,1280]{1,0:T(8,128)(2,1)S(1)}, u32[]{:S(2)}, u32[]{:S(2)}) collective-permute-start(bf16[104,1280]{1,0:T(8,128)(2,1)S(1)} %get-tuple-element.91), channel_id=1, source_target_pairs={{0,14},{1,15},{2,0},{3,1},{4,2},{5,3},{6,4},{7,5},{8,6},{9,7},{10,... | collective-permute-start | bytes 798728 | tf_op jit(solution)/shard_map/ppermute | solution.py:299
  69.0 12.2 %collective-permute-start.5 = (bf16[104,1280]{1,0:T(8,128)(2,1)S(1)}, bf16[104,1280]{1,0:T(8,128)(2,1)S(1)}, u32[]{:S(2)}, u32[]{:S(2)}) collective-permute-start(bf16[104,1280]{1,0:T(8,128)(2,1)S(1)} %get-tuple-element.90), channel_id=1, source_target_pairs={{0,2},{1,3},{2,4},{3,5},{4,6},{5,7},{6,8},{7,9},{8,10},{9,11},{10,... | collective-permute-start | bytes 798728 | tf_op jit(solution)/shard_map/ppermute | solution.py:299
  70.5 10.3 %collective-permute-start.18 = (bf16[104,1152]{1,0:T(8,128)(2,1)S(1)}, bf16[104,1152]{1,0:T(8,128)(2,1)S(1)}, u32[]{:S(2)}, u32[]{:S(2)}) collective-permute-start(bf16[104,1152]{1,0:T(8,128)(2,1)S(1)} %fusion.7), channel_id=1, source_target_pairs={{0,14},{1,15},{2,0},{3,1},{4,2},{5,3},{6,4},{7,5},{8,6},{9,7},{10,... | collective-permute-start | bytes 718856 | tf_op jit(solution)/shard_map/ppermute | solution.py:299
  77.5 6.2 %collective-permute-start.9 = (bf16[104,1280]{1,0:T(8,128)(2,1)S(1)}, bf16[104,1280]{1,0:T(8,128)(2,1)S(1)}, u32[]{:S(2)}, u32[]{:S(2)}) collective-permute-start(bf16[104,1280]{1,0:T(8,128)(2,1)S(1)} %fusion.1), channel_id=1, source_target_pairs={{0,14},{1,15},{2,0},{3,1},{4,2},{5,3},{6,4},{7,5},{8,6},{9,7},{10,... | collective-permute-start | bytes 798728 | tf_op jit(solution)/shard_map/ppermute | solution.py:299
  80.9 5.4 %collective-permute-start.19 = (bf16[104,1152]{1,0:T(8,128)(2,1)S(1)}, bf16[104,1152]{1,0:T(8,128)(2,1)S(1)}, u32[]{:S(2)}, u32[]{:S(2)}) collective-permute-start(bf16[104,1152]{1,0:T(8,128)(2,1)S(1)} %fusion.11), channel_id=1, source_target_pairs={{0,1},{1,0},{2,3},{3,2},{4,5},{5,4},{6,7},{7,6},{8,9},{9,8},{10,11... | collective-permute-start | bytes 718856 | tf_op jit(solution)/shard_map/ppermute | solution.py:303
  83.8 5.4 %collective-permute-start.10 = (bf16[104,1280]{1,0:T(8,128)(2,1)S(1)}, bf16[104,1280]{1,0:T(8,128)(2,1)S(1)}, u32[]{:S(2)}, u32[]{:S(2)}) collective-permute-start(bf16[104,1280]{1,0:T(8,128)(2,1)S(1)} %fusion.5), channel_id=1, source_target_pairs={{0,1},{1,0},{2,3},{3,2},{4,5},{5,4},{6,7},{7,6},{8,9},{9,8},{10,11... | collective-permute-start | bytes 798728 | tf_op jit(solution)/shard_map/ppermute | solution.py:303
  86.3 6.8 %copy-start.1 = (bf16[1,2432,448]{1,2,0:T(8,128)(2,1)S(1)}, bf16[1,2432,448]{1,2,0:T(8,128)(2,1)}, u32[]{:S(2)}) copy-start(bf16[1,2432,448]{1,2,0:T(8,128)(2,1)} %param.17) | copy-start | bytes 6537220
  86.3 6.8 %copy-start = (bf16[1,448,2432]{2,1,0:T(8,128)(2,1)S(1)}, bf16[1,448,2432]{2,1,0:T(8,128)(2,1)}, u32[]{:S(2)}) copy-start(bf16[1,448,2432]{2,1,0:T(8,128)(2,1)} %param.16) | copy-start | bytes 6537220
  89.5 8.2 %collective-permute-start.20 = (bf16[72,2432]{1,0:T(8,128)(2,1)S(1)}, bf16[72,2432]{1,0:T(8,128)(2,1)S(1)}, u32[]{:S(2)}, u32[]{:S(2)}) collective-permute-start(bf16[72,2432]{1,0:T(8,128)(2,1)S(1)} %maximum_maximum_fusion.refs_0_), channel_id=1, source_target_pairs={{0,2},{1,3},{2,4},{3,5},{4,6},{5,7},{6,8},{7,9},{8,10},{9,11},{10,... | collective-permute-start | bytes 1050632 | tf_op jit(solution)/shard_map/ppermute | solution.py:299
  90.4 10.7 %collective-permute-start.21 = (bf16[72,2432]{1,0:T(8,128)(2,1)S(1)}, bf16[72,2432]{1,0:T(8,128)(2,1)S(1)}, u32[]{:S(2)}, u32[]{:S(2)}) collective-permute-start(bf16[72,2432]{1,0:T(8,128)(2,1)S(1)} %maximum_maximum_fusion.refs_0_), channel_id=1, source_target_pairs={{0,14},{1,15},{2,0},{3,1},{4,2},{5,3},{6,4},{7,5},{8,6},{9,7},{10,... | collective-permute-start | bytes 1050632 | tf_op jit(solution)/shard_map/ppermute | solution.py:299
  101.2 7.4 %collective-permute-start.22 = (bf16[72,2432]{1,0:T(8,128)(2,1)S(1)}, bf16[72,2432]{1,0:T(8,128)(2,1)S(1)}, u32[]{:S(2)}, u32[]{:S(2)}) collective-permute-start(bf16[72,2432]{1,0:T(8,128)(2,1)S(1)} %collective-permute-done.20.refs_0_), channel_id=1, source_target_pairs={{0,2},{1,3},{2,4},{3,5},{4,6},{5,7},{6,8},{7,9},{8,10},{9,11},{10,... | collective-permute-start | bytes 1050632 | tf_op jit(solution)/shard_map/ppermute | solution.py:299
  101.7 6.9 %collective-permute-start.23 = (bf16[72,2432]{1,0:T(8,128)(2,1)S(1)}, bf16[72,2432]{1,0:T(8,128)(2,1)S(1)}, u32[]{:S(2)}, u32[]{:S(2)}) collective-permute-start(bf16[72,2432]{1,0:T(8,128)(2,1)S(1)} %collective-permute-done.21.refs_1_), channel_id=1, source_target_pairs={{0,14},{1,15},{2,0},{3,1},{4,2},{5,3},{6,4},{7,5},{8,6},{9,7},{10,... | collective-permute-start | bytes 1050632 | tf_op jit(solution)/shard_map/ppermute | solution.py:299
  108.6 12.1 %collective-permute-start.24 = (bf16[72,2432]{1,0:T(8,128)(2,1)S(1)}, bf16[72,2432]{1,0:T(8,128)(2,1)S(1)}, u32[]{:S(2)}, u32[]{:S(2)}) collective-permute-start(bf16[72,2432]{1,0:T(8,128)(2,1)S(1)} %collective-permute-done.22.refs_0_), channel_id=1, source_target_pairs={{0,2},{1,3},{2,4},{3,5},{4,6},{5,7},{6,8},{7,9},{8,10},{9,11},{10,... | collective-permute-start | bytes 1050632 | tf_op jit(solution)/shard_map/ppermute | solution.py:299
  109.5 11.1 %collective-permute-start.25 = (bf16[72,2432]{1,0:T(8,128)(2,1)S(1)}, bf16[72,2432]{1,0:T(8,128)(2,1)S(1)}, u32[]{:S(2)}, u32[]{:S(2)}) collective-permute-start(bf16[72,2432]{1,0:T(8,128)(2,1)S(1)} %collective-permute-done.23.refs_1_), channel_id=1, source_target_pairs={{0,14},{1,15},{2,0},{3,1},{4,2},{5,3},{6,4},{7,5},{8,6},{9,7},{10,... | collective-permute-start | bytes 1050632 | tf_op jit(solution)/shard_map/ppermute | solution.py:299
  111.2 9.3 %collective-permute-start.26 = (bf16[72,448]{1,0:T(8,128)(2,1)S(1)}, bf16[72,448]{1,0:T(8,128)(2,1)S(1)}, u32[]{:S(2)}, u32[]{:S(2)}) collective-permute-start(bf16[72,448]{1,0:T(8,128)(2,1)S(1)} %get-tuple-element.67), channel_id=1, source_target_pairs={{0,14},{1,15},{2,0},{3,1},{4,2},{5,3},{6,4},{7,5},{8,6},{9,7},{10,... | collective-permute-start | bytes 193544 | tf_op jit(solution)/shard_map/ppermute | solution.py:299
  112.7 8.0 %collective-permute-start.27 = (bf16[72,448]{1,0:T(8,128)(2,1)S(1)}, bf16[72,448]{1,0:T(8,128)(2,1)S(1)}, u32[]{:S(2)}, u32[]{:S(2)}) collective-permute-start(bf16[72,448]{1,0:T(8,128)(2,1)S(1)} %get-tuple-element.68), channel_id=1, source_target_pairs={{0,2},{1,3},{2,4},{3,5},{4,6},{5,7},{6,8},{7,9},{8,10},{9,11},{10,... | collective-permute-start | bytes 193544 | tf_op jit(solution)/shard_map/ppermute | solution.py:299
  120.7 11.0 %collective-permute-start.29 = (bf16[40,2432]{1,0:T(8,128)(2,1)S(1)}, bf16[40,2432]{1,0:T(8,128)(2,1)S(1)}, u32[]{:S(2)}, u32[]{:S(2)}) collective-permute-start(bf16[40,2432]{1,0:T(8,128)(2,1)S(1)} %slice.103), channel_id=1, source_target_pairs={{0,14},{1,15},{2,0},{3,1},{4,2},{5,3},{6,4},{7,5},{8,6},{9,7},{10,... | collective-permute-start | bytes 583688 | tf_op jit(solution)/shard_map/ppermute | solution.py:299
  123.2 8.6 %collective-permute-start.28 = (bf16[32,2432]{1,0:T(8,128)(2,1)S(1)}, bf16[32,2432]{1,0:T(8,128)(2,1)S(1)}, u32[]{:S(2)}, u32[]{:S(2)}) collective-permute-start(bf16[32,2432]{1,0:T(8,128)(2,1)S(1)} %slice.102), channel_id=1, source_target_pairs={{0,2},{1,3},{2,4},{3,5},{4,6},{5,7},{6,8},{7,9},{8,10},{9,11},{10,... | collective-permute-start | bytes 466952 | tf_op jit(solution)/shard_map/ppermute | solution.py:299
  123.3 7.5 %collective-permute-start.30 = (bf16[72,448]{1,0:T(8,128)(2,1)S(1)}, bf16[72,448]{1,0:T(8,128)(2,1)S(1)}, u32[]{:S(2)}, u32[]{:S(2)}) collective-permute-start(bf16[72,448]{1,0:T(8,128)(2,1)S(1)} %get-tuple-element.71), channel_id=1, source_target_pairs={{0,12},{1,13},{2,14},{3,15},{4,0},{5,1},{6,2},{7,3},{8,4},{9,5},{1... | collective-permute-start | bytes 193544 | tf_op jit(solution)/shard_map/ppermute | solution.py:299
  124.8 6.9 %collective-permute-start.31 = (bf16[72,448]{1,0:T(8,128)(2,1)S(1)}, bf16[72,448]{1,0:T(8,128)(2,1)S(1)}, u32[]{:S(2)}, u32[]{:S(2)}) collective-permute-start(bf16[72,448]{1,0:T(8,128)(2,1)S(1)} %get-tuple-element.72), channel_id=1, source_target_pairs={{0,4},{1,5},{2,6},{3,7},{4,8},{5,9},{6,10},{7,11},{8,12},{9,13},{1... | collective-permute-start | bytes 193544 | tf_op jit(solution)/shard_map/ppermute | solution.py:299
  128.4 8.6 %collective-permute-start.32 = (bf16[72,448]{1,0:T(8,128)(2,1)S(1)}, bf16[72,448]{1,0:T(8,128)(2,1)S(1)}, u32[]{:S(2)}, u32[]{:S(2)}) collective-permute-start(bf16[72,448]{1,0:T(8,128)(2,1)S(1)} %get-tuple-element.76), channel_id=1, source_target_pairs={{0,10},{1,11},{2,12},{3,13},{4,14},{5,15},{6,0},{7,1},{8,2},{9,3},... | collective-permute-start | bytes 193544 | tf_op jit(solution)/shard_map/ppermute | solution.py:299
  130.8 7.5 %collective-permute-start.34 = (bf16[72,448]{1,0:T(8,128)(2,1)S(1)}, bf16[72,448]{1,0:T(8,128)(2,1)S(1)}, u32[]{:S(2)}, u32[]{:S(2)}) collective-permute-start(bf16[72,448]{1,0:T(8,128)(2,1)S(1)} %get-tuple-element.77), channel_id=1, source_target_pairs={{0,6},{1,7},{2,8},{3,9},{4,10},{5,11},{6,12},{7,13},{8,14},{9,15},... | collective-permute-start | bytes 193544 | tf_op jit(solution)/shard_map/ppermute | solution.py:299
  131.8 10.4 %copy-start.2 = (f32[8,128]{1,0:T(8,128)S(1)}, f32[8,128]{1,0:T(8,128)}, u32[]{:S(2)}) copy-start(f32[8,128]{1,0:T(8,128)} %get-tuple-element.57.meta) | copy-start | bytes 12292
  133.1 9.1 %collective-permute-start.33 = (bf16[72,448]{1,0:T(8,128)(2,1)S(1)}, bf16[72,448]{1,0:T(8,128)(2,1)S(1)}, u32[]{:S(2)}, u32[]{:S(2)}) collective-permute-start(bf16[72,448]{1,0:T(8,128)(2,1)S(1)} %outward.9), channel_id=1, source_target_pairs={{0,8},{1,9},{2,10},{3,11},{4,12},{5,13},{6,14},{7,15},{8,0},{9,1},... | collective-permute-start | bytes 193544 | tf_op jit(solution)/shard_map/ppermute | solution.py:299
  144.2 32.4 %collective-permute-start.35 = (bf16[8,24,448]{2,1,0:T(8,128)(2,1)S(1)}, bf16[8,24,448]{2,1,0:T(8,128)(2,1)S(1)}, u32[]{:S(2)}, u32[]{:S(2)}) collective-permute-start(bf16[8,24,448]{2,1,0:T(8,128)(2,1)S(1)} %get-tuple-element.83), channel_id=1, source_target_pairs={{0,16},{1,17},{2,18},{3,19},{4,20},{5,21},{6,22},{7,23},{8,24},{9,... | collective-permute-start | bytes 516104 | tf_op jit(solution)/shard_map/ppermute | solution.py:313
  171.6 6.7 %collective-permute-start.36 = (bf16[8,24,448]{2,1,0:T(8,128)(2,1)S(1)}, bf16[8,24,448]{2,1,0:T(8,128)(2,1)S(1)}, u32[]{:S(2)}, u32[]{:S(2)}) collective-permute-start(bf16[8,24,448]{2,1,0:T(8,128)(2,1)S(1)} %get-tuple-element.84), channel_id=1, source_target_pairs={{0,17},{1,16},{2,19},{3,18},{4,21},{5,20},{6,23},{7,22},{8,25},{9,... | collective-permute-start | bytes 516104 | tf_op jit(solution)/shard_map/ppermute | solution.py:313
  171.6 6.7 %collective-permute-start.37 = (bf16[8,24,448]{2,1,0:T(8,128)(2,1)S(1)}, bf16[8,24,448]{2,1,0:T(8,128)(2,1)S(1)}, u32[]{:S(2)}, u32[]{:S(2)}) collective-permute-start(bf16[8,24,448]{2,1,0:T(8,128)(2,1)S(1)} %get-tuple-element.86), channel_id=1, source_target_pairs={{0,240},{1,241},{2,242},{3,243},{4,244},{5,245},{6,246},{7,247},{8... | collective-permute-start | bytes 516104 | tf_op jit(solution)/shard_map/ppermute | solution.py:313
  171.8 11.9 %collective-permute-start.38 = (bf16[8,24,448]{2,1,0:T(8,128)(2,1)S(1)}, bf16[8,24,448]{2,1,0:T(8,128)(2,1)S(1)}, u32[]{:S(2)}, u32[]{:S(2)}) collective-permute-start(bf16[8,24,448]{2,1,0:T(8,128)(2,1)S(1)} %get-tuple-element.87), channel_id=1, source_target_pairs={{0,241},{1,240},{2,243},{3,242},{4,245},{5,244},{6,247},{7,246},{8... | collective-permute-start | bytes 516104 | tf_op jit(solution)/shard_map/ppermute | solution.py:313
where the time goes:
time: 189 us; the launch traced here: 188 us
  starting transfers between devices  81.5 us (43%)
  waiting for transfers between devices  74.3 us (39%)
  Pallas kernels  29.9 us (16%)
    ppermute x31, waiting for transfers between devices, around(): return lax.ppermute(value, 'expert', pairs)  43.3 us
    ppermute x31, starting transfers between devices, around(): return lax.ppermute(value, 'expert', pairs)  36.4 us
    ppermute x6, starting transfers between devices, section_shift(): return lax.ppermute(value, ('section', 'expert'), pairs)  35.8 us
    all_to_all x1, waiting for transfers between devices, per_device(): lax.all_to_all(packed, 'expert', split_axis=0, concat_axis=0, tiled=True)  19.1 us
    pallas_call x5, Pallas kernels, outward(): pl.pallas_call(functools.partial(outward_kernel, count), out_shape=[jax.S...  10.7 us
    all_to_all x1, starting transfers between devices, per_device(): lax.all_to_all(packed, 'expert', split_axis=0, concat_axis=0, tiled=True)  8.59 us
    ppermute x6, waiting for transfers between devices, section_shift(): return lax.ppermute(value, ('section', 'expert'), pairs)  7.08 us
    pallas_call x1, Pallas kernels, partial_sums(): pl.pallas_call(partial_kernel, out_shape=shapes, in_specs=[pl.BlockSpec(m...  6.84 us
  transfers between devices with their start and end apart: 40, of which 20 were waited for; matrix products, arithmetic and copies ran while one was open for 1% of the time, Pallas kernels for 9%

commit v1 on v0

--- a/solution.py
+++ b/solution.py
@@ -21,7 +21,7 @@
 BF = jnp.bfloat16
 F32 = jnp.float32
 WIDE = 2 * COLS
-VMEM_LIMIT = 48 * 1024 * 1024
+VMEM_LIMIT = 24 * 1024 * 1024
 VMEM_MOST = 60 * 1024 * 1024
 STREAMS = (slice(0, FIRST), slice(FIRST, FF))
 CUT = 48
@@ -216,9 +216,7 @@
 
 
 def settle_kernel(place, meta, *refs):
-    parts, outs, held = refs[:NODES], refs[NODES:-1], refs[-1]
-    for k, part in enumerate(parts):
-        held[k] = part[...]
+    parts, outs = refs[:NODES], refs[NODES:]
     r, c = iota((ROWS, SENT), 0), iota((ROWS, SENT), 1)
     line = iota((ROWS, COLS), 0)
     heads = []
@@ -227,15 +225,16 @@
         for at, source in rows:
             head = jnp.where(line[:, :TOK] == at, meta[source : source + 1, :], head)
         heads.append(jnp.concatenate([head, jnp.zeros((ROWS, COLS - TOK), F32)], axis=1))
+    even = place[2] == 0
     picks = []
-    for start, head in ((0, heads[0]), (2 * MOST, heads[1])):
+    for forward in (even, jnp.logical_not(even)):
+        start = jnp.where(forward, 0, 2 * MOST)
+        head = jnp.where(forward, heads[0], heads[1])
         for owner in (place[1], 1 - place[1]):
             picks.append((onehot((r < MOST) & (c == r + start + owner * MOST)), head))
-
-    @pl.loop(0, NODES)
-    def _(k):
+    for k, part in enumerate(parts):
         at = lax.rem(place[0] + k, NODES)
-        rows = held[k]
+        rows = part[...]
         for (select, head), out in zip(picks, outs):
             out[at] = (dot(select, rows) + head).astype(BF)
 
@@ -247,14 +246,16 @@
         out_shape=(jax.ShapeDtypeStruct((NODES, ROWS, COLS), BF),) * 4,
         in_specs=[pl.BlockSpec(memory_space=pltpu.SMEM)] + [vmem] * (NODES + 1),
         out_specs=(vmem,) * 4,
-        scratch_shapes=[pltpu.VMEM((NODES, SENT, COLS), BF)],
         compiler_params=pltpu.CompilerParams(vmem_limit_bytes=VMEM_LIMIT),
         name="settle",
     )(place, meta, *parts)
 
 
-def patch_kernel(place, fraw, fown, fother, braw, bown, bother, fout, bout):
-    first = place[1] == 0
+def patch_kernel(place, fraw, braw, far, far_other, near, near_other, fout, bout):
+    first, even = place[1] == 0, place[2] == 0
+    near, near_other, far, far_other = near[...], near_other[...], far[...], far_other[...]
+    fown, fother = jnp.where(even, far, near), jnp.where(even, far_other, near_other)
+    bown, bother = jnp.where(even, near, far), jnp.where(even, near_other, far_other)
     line = iota((ROWS, TOK), 0)
     ones = jnp.ones((ROWS, TOK), BF)
     for raw, own, other, out, scaled in (
@@ -279,7 +280,7 @@
             out[:, cols] = (raw[:, cols].astype(F32) + fresh).astype(BF)
 
 
-def patch(place, fraw, fown, fother, braw, bown, bother):
+def patch(place, fraw, braw, *rows_sent):
     steps = 4
     strip = pl.BlockSpec((TOK, D // steps), lambda i: (0, i))
     rows = pl.BlockSpec((NODES // steps, ROWS, COLS), lambda i: (i, 0, 0))
@@ -287,11 +288,11 @@
         patch_kernel,
         grid=(steps,),
         out_shape=(jax.ShapeDtypeStruct((TOK, D), BF),) * 2,
-        in_specs=[pl.BlockSpec(memory_space=pltpu.SMEM), strip, rows, rows, strip, rows, rows],
+        in_specs=[pl.BlockSpec(memory_space=pltpu.SMEM), strip, strip] + [rows] * 4,
         out_specs=(strip, strip),
         compiler_params=pltpu.CompilerParams(vmem_limit_bytes=VMEM_LIMIT),
         name="patch",
-    )(place, fraw, fown, fother, braw, bown, bother)
+    )(place, fraw, braw, *rows_sent)
 
 
 def around(value, steps):
@@ -303,10 +304,10 @@
     return lax.ppermute(value, "expert", [(e, e ^ 1) for e in range(2 * NODES)])
 
 
-def section_shift(value, steps, flip=0):
+def section_move(value, target, flip=0):
     sections, experts = lax.axis_size("section"), lax.axis_size("expert")
     pairs = [
-        (s * experts + e, (s + steps) % sections * experts + (e ^ flip))
+        (s * experts + e, target(s) % sections * experts + (e ^ flip))
         for s in range(sections)
         for e in range(experts)
     ]
@@ -376,7 +377,8 @@
 ):
     up, down = up_weight[0], down_weight[0].T
     expert = lax.axis_index("expert").astype(jnp.int32)
-    place = jnp.stack([expert // 2, expert % 2])
+    section = lax.axis_index("section").astype(jnp.int32)
+    place = jnp.stack([expert // 2, expert % 2, section % 2])
     packed, meta = pick(
         forward_routes[0].T,
         forward_gates[0].T,
@@ -388,23 +390,19 @@
     )
     packed, acts, cot = lax.optimization_barrier((packed, forward_in[0], backward_grad[0]))
     picks = lax.all_to_all(packed, "expert", split_axis=0, concat_axis=0, tiled=True)
-    fraw, braw = section_shift(acts, 1), section_shift(cot, -1)
+    fraw, braw = section_move(acts, lambda s: s + 1), section_move(cot, lambda s: s - 1)
     (right1, left1, right2, left2, part1, part2), fraw, braw = lax.optimization_barrier(
         (partial_sums(place, picks, up, down), fraw, braw)
     )
     totals = [scatter_ring(right1, left1, part1), scatter_ring(right2, left2, part2)]
     mine = jnp.concatenate([activate(total) for total in totals], axis=1)
     back = gather_ring(mine, up, down)
-    fown, fother, bown, bother = settle(place, meta, back)
-    forward_out, backward_out = patch(
-        place,
-        fraw,
-        section_shift(fown, 1),
-        section_shift(fother, 1, 1),
-        braw,
-        section_shift(bown, -1),
-        section_shift(bother, -1, 1),
-    )
+    near, near_other, far, far_other = settle(place, meta, back)
+    beside = lambda s: s ^ 1
+    beyond = lambda s: s + 1 if s % 2 else s - 1
+    far, far_other = section_move(far, beyond), section_move(far_other, beyond, 1)
+    near, near_other = section_move(near, beside), section_move(near_other, beside, 1)
+    forward_out, backward_out = patch(place, fraw, braw, far, far_other, near, near_other)
     return forward_out[None], backward_out[None]
 
 

time: 189 us -> 187 us (0.989)
  Pallas kernels: 29.9 us -> 27.8 us
  transfers between devices with their start and end apart: 40 -> 40, of which waited for: 20 -> 20; matrix products, arithmetic and copies ran while one was open for 1% -> 1% of each run, Pallas kernels for 9% -> 8%
where the time goes in v1:
time: 187 us
  starting transfers between devices  81.1 us (43%)
  waiting for transfers between devices  73.7 us (39%)
  Pallas kernels  27.8 us (15%)
    ppermute x31, waiting for transfers between devices, around(): return lax.ppermute(value, 'expert', pairs)  43.1 us
    ppermute x31, starting transfers between devices, around(): return lax.ppermute(value, 'expert', pairs)  36.5 us
    ppermute x6, starting transfers between devices, section_move(): return lax.ppermute(value, ('section', 'expert'), pairs)  35.3 us
    all_to_all x1, waiting for transfers between devices, per_device(): lax.all_to_all(packed, 'expert', split_axis=0, concat_axis=0, tiled=True)  19.1 us
    pallas_call x5, Pallas kernels, outward(): pl.pallas_call(functools.partial(outward_kernel, count), out_shape=[jax.S...  10.7 us
    all_to_all x1, starting transfers between devices, per_device(): lax.all_to_all(packed, 'expert', split_axis=0, concat_axis=0, tiled=True)  8.57 us
    ppermute x6, waiting for transfers between devices, section_move(): return lax.ppermute(value, ('section', 'expert'), pairs)  6.52 us
    pallas_call x1, Pallas kernels, pick(): pl.pallas_call(pick_kernel, in_specs=[vmem] * 4 + [anywhere] * 3, out_spe...  5.89 us
  transfers between devices with their start and end apart: 40, of which 20 were waited for; matrix products, arithmetic and copies ran while one was open for 1% of the time, Pallas kernels for 8%

profile of v1, /device:TPU:1, one launch (start us, length us, event | category | flops | bytes accessed | tf_op | source)
XLA Modules:
  0.0 186.8 jit_solution(1114900638115008913)
XLA Ops:
  0.6 5.9 %pick.1 = (bf16[16,56,448]{2,1,0:T(8,128)(2,1)}, f32[8,128]{1,0:T(8,128)}) custom-call(s32[2,128]{1,0:T(2,128)} %bitcast.91, f32[2,128]{1,0:T(2,128)} %bitcast.92, s32[2,128]{1,0:T(2,128)} %bitcast.93, f32[2,128]{1,0:T(2,128)} %bitcast.94, bf16[128,7168]{1,0:T(8,128)(2,1)} %bitcast.87, bf16[128,7168]{1,0:T(8,128)(2,1)} %bitcast.86, bf16[128,7168]{1,0:T(8,128)(2,1)} %bitcast.89), custom_call_target="tpu_custom_call" | custom-call | tf_op jit(solution)/shard_map/pick/pallas_call | solution.py:109
  6.5 2.8 %collective-permute-start = (bf16[128,7168]{1,0:T(8,128)(2,1)}, bf16[128,7168]{1,0:T(8,128)(2,1)}, u32[]{:S(2)}, u32[]{:S(2)}) collective-permute-start(bf16[128,7168]{1,0:T(8,128)(2,1)} %bitcast.88), channel_id=1, source_target_pairs={{0,16},{1,17},{2,18},{3,19},{4,20},{5,21},{6,22},{7,23},{8,24},{9,... | collective-permute-start | bytes 5505032 | tf_op jit(solution)/shard_map/ppermute | solution.py:314
  10.0 8.6 %all-to-all-start = ((bf16[16,56,448]{2,1,0:T(8,128)(2,1)}), bf16[16,56,448]{2,1,0:T(8,128)(2,1)S(1)}, u32[]{:S(2)}, u32[]{:S(2)}) async-start(bf16[16,56,448]{2,1,0:T(8,128)(2,1)} %get-tuple-element.47), calls=%async_computation | async-start | bytes 1835008 | tf_op jit(solution)/shard_map/all_to_all | solution.py:392
  18.6 19.1 %all-to-all-done.picks = bf16[16,56,448]{2,1,0:T(8,128)(2,1)S(1)} async-done(((bf16[16,56,448]{2,1,0:T(8,128)(2,1)}), bf16[16,56,448]{2,1,0:T(8,128)(2,1)S(1)}, u32[]{:S(2)}, u32[]{:S(2)}) %all-to-all-start) | async-done | bytes 802848 | tf_op jit(solution)/shard_map/all_to_all | solution.py:392
  37.8 1.6 copy-done.1
  39.4 5.1 %partials.1 = (bf16[48,1280]{1,0:T(8,128)(2,1)S(1)}, bf16[56,1280]{1,0:T(8,128)(2,1)S(1)}, bf16[48,1152]{1,0:T(8,128)(2,1)S(1)}, bf16[56,1152]{1,0:T(8,128)(2,1)...) custom-call(s32[3]{0:T(128)S(1)} %pad_add_fusion.place, ...), custom_call_target="tpu_custom_call" | custom-call | tf_op jit(solution)/shard_map/partials/pallas_call | solution.py:173
  44.8 2.6 %collective-permute-start.15 = (bf16[56,1152]{1,0:T(8,128)(2,1)S(1)}, bf16[56,1152]{1,0:T(8,128)(2,1)S(1)}, u32[]{:S(2)}, u32[]{:S(2)}) collective-permute-start(bf16[56,1152]{1,0:T(8,128)(2,1)S(1)} %get-tuple-element.64), channel_id=1, source_target_pairs={{0,14},{1,15},{2,0},{3,1},{4,2},{5,3},{6,4},{7,5},{8,6},{9,7},{10,... | collective-permute-start | bytes 387080 | tf_op jit(solution)/shard_map/ppermute | solution.py:300
  47.5 2.7 %collective-permute-start.6 = (bf16[56,1280]{1,0:T(8,128)(2,1)S(1)}, bf16[56,1280]{1,0:T(8,128)(2,1)S(1)}, u32[]{:S(2)}, u32[]{:S(2)}) collective-permute-start(bf16[56,1280]{1,0:T(8,128)(2,1)S(1)} %get-tuple-element.61), channel_id=1, source_target_pairs={{0,14},{1,15},{2,0},{3,1},{4,2},{5,3},{6,4},{7,5},{8,6},{9,7},{10,... | collective-permute-start | bytes 430088 | tf_op jit(solution)/shard_map/ppermute | solution.py:300
  50.3 2.1 %collective-permute-done.2 = bf16[48,1280]{1,0:T(8,128)(2,1)S(1)} collective-permute-done((bf16[48,1280]{1,0:T(8,128)(2,1)S(1)}, bf16[48,1280]{1,0:T(8,128)(2,1)S(1)}, u32[]{:S(2)}, u32[]{:S(2)}) %collective-permute-start.2) | collective-permute-done | bytes 122912 | tf_op jit(solution)/shard_map/ppermute | solution.py:300
  52.6 2.7 %collective-permute-start.16 = (bf16[104,1152]{1,0:T(8,128)(2,1)S(1)}, bf16[104,1152]{1,0:T(8,128)(2,1)S(1)}, u32[]{:S(2)}, u32[]{:S(2)}) collective-permute-start(bf16[104,1152]{1,0:T(8,128)(2,1)S(1)} %pad_maximum_fusion.4), channel_id=1, source_target_pairs={{0,14},{1,15},{2,0},{3,1},{4,2},{5,3},{6,4},{7,5},{8,6},{9,7},{10,... | collective-permute-start | bytes 718856 | tf_op jit(solution)/shard_map/ppermute | solution.py:300
  57.1 2.2 %collective-permute-done.3 = bf16[104,1280]{1,0:T(8,128)(2,1)S(1)} collective-permute-done((bf16[104,1280]{1,0:T(8,128)(2,1)S(1)}, bf16[104,1280]{1,0:T(8,128)(2,1)S(1)}, u32[]{:S(2)}, u32[]{:S(2)}) %collective-permute-start.3) | collective-permute-done | bytes 266272 | tf_op jit(solution)/shard_map/ppermute | solution.py:300
  59.5 4.7 %collective-permute-done.13 = bf16[104,1152]{1,0:T(8,128)(2,1)S(1)} collective-permute-done((bf16[104,1152]{1,0:T(8,128)(2,1)S(1)}, bf16[104,1152]{1,0:T(8,128)(2,1)S(1)}, u32[]{:S(2)}, u32[]{:S(2)}) %collective-permute-start.13) | collective-permute-done | bytes 239648 | tf_op jit(solution)/shard_map/ppermute | solution.py:300
  64.5 1.5 collective-permute-start.14
  65.9 3.0 %collective-permute-done.4 = bf16[104,1280]{1,0:T(8,128)(2,1)S(1)} collective-permute-done((bf16[104,1280]{1,0:T(8,128)(2,1)S(1)}, bf16[104,1280]{1,0:T(8,128)(2,1)S(1)}, u32[]{:S(2)}, u32[]{:S(2)}) %collective-permute-start.4) | collective-permute-done | bytes 266272 | tf_op jit(solution)/shard_map/ppermute | solution.py:300
  69.2 1.5 collective-permute-start.5
  70.7 1.4 collective-permute-start.18
  72.1 5.4 %collective-permute-done.8 = bf16[104,1280]{1,0:T(8,128)(2,1)S(1)} collective-permute-done((bf16[104,1280]{1,0:T(8,128)(2,1)S(1)}, bf16[104,1280]{1,0:T(8,128)(2,1)S(1)}, u32[]{:S(2)}, u32[]{:S(2)}) %collective-permute-start.8) | collective-permute-done | bytes 266272 | tf_op jit(solution)/shard_map/ppermute | solution.py:300
  77.7 3.2 %collective-permute-done.18 = bf16[104,1152]{1,0:T(8,128)(2,1)S(1)} collective-permute-done((bf16[104,1152]{1,0:T(8,128)(2,1)S(1)}, bf16[104,1152]{1,0:T(8,128)(2,1)S(1)}, u32[]{:S(2)}, u32[]{:S(2)}) %collective-permute-start.18) | collective-permute-done | bytes 239648 | tf_op jit(solution)/shard_map/ppermute | solution.py:300
  81.4 2.4 %collective-permute-done.9 = bf16[104,1280]{1,0:T(8,128)(2,1)S(1)} collective-permute-done((bf16[104,1280]{1,0:T(8,128)(2,1)S(1)}, bf16[104,1280]{1,0:T(8,128)(2,1)S(1)}, u32[]{:S(2)}, u32[]{:S(2)}) %collective-permute-start.9) | collective-permute-done | bytes 266272 | tf_op jit(solution)/shard_map/ppermute | solution.py:300
  84.2 2.2 %collective-permute-done.19 = bf16[104,1152]{1,0:T(8,128)(2,1)S(1)} collective-permute-done((bf16[104,1152]{1,0:T(8,128)(2,1)S(1)}, bf16[104,1152]{1,0:T(8,128)(2,1)S(1)}, u32[]{:S(2)}, u32[]{:S(2)}) %collective-permute-start.19) | collective-permute-done | bytes 239648 | tf_op jit(solution)/shard_map/ppermute | solution.py:304
  86.6 2.7 %collective-permute-done.10 = bf16[104,1280]{1,0:T(8,128)(2,1)S(1)} collective-permute-done((bf16[104,1280]{1,0:T(8,128)(2,1)S(1)}, bf16[104,1280]{1,0:T(8,128)(2,1)S(1)}, u32[]{:S(2)}, u32[]{:S(2)}) %collective-permute-start.10) | collective-permute-done | bytes 266272 | tf_op jit(solution)/shard_map/ppermute | solution.py:304
  90.4 2.9 %collective-permute-start.21 = (bf16[72,2432]{1,0:T(8,128)(2,1)S(1)}, bf16[72,2432]{1,0:T(8,128)(2,1)S(1)}, u32[]{:S(2)}, u32[]{:S(2)}) collective-permute-start(bf16[72,2432]{1,0:T(8,128)(2,1)S(1)} %maximum_maximum_fusion.refs_0_), channel_id=1, source_target_pairs={{0,14},{1,15},{2,0},{3,1},{4,2},{5,3},{6,4},{7,5},{8,6},{9,7},{10,... | collective-permute-start | bytes 1050632 | tf_op jit(solution)/shard_map/ppermute | solution.py:300
  93.3 1.3 outward.5.refs_0_
  94.6 3.3 %collective-permute-done.20.refs_0_ = bf16[72,2432]{1,0:T(8,128)(2,1)S(1)} collective-permute-done((bf16[72,2432]{1,0:T(8,128)(2,1)S(1)}, bf16[72,2432]{1,0:T(8,128)(2,1)S(1)}, u32[]{:S(2)}, u32[]{:S(2)}) %collective-permute-start.20) | collective-permute-done | bytes 350240 | tf_op jit(solution)/shard_map/ppermute | solution.py:300
  97.9 3.5 %collective-permute-done.21.refs_1_ = bf16[72,2432]{1,0:T(8,128)(2,1)S(1)} collective-permute-done((bf16[72,2432]{1,0:T(8,128)(2,1)S(1)}, bf16[72,2432]{1,0:T(8,128)(2,1)S(1)}, u32[]{:S(2)}, u32[]{:S(2)}) %collective-permute-start.21) | collective-permute-done | bytes 350240 | tf_op jit(solution)/shard_map/ppermute | solution.py:300
  101.8 2.3 %collective-permute-start.23 = (bf16[72,2432]{1,0:T(8,128)(2,1)S(1)}, bf16[72,2432]{1,0:T(8,128)(2,1)S(1)}, u32[]{:S(2)}, u32[]{:S(2)}) collective-permute-start(bf16[72,2432]{1,0:T(8,128)(2,1)S(1)} %collective-permute-done.21.refs_1_), channel_id=1, source_target_pairs={{0,14},{1,15},{2,0},{3,1},{4,2},{5,3},{6,4},{7,5},{8,6},{9,7},{10,... | collective-permute-start | bytes 1050632 | tf_op jit(solution)/shard_map/ppermute | solution.py:300
  104.1 2.7 %outward.6 = (bf16[72,448]{1,0:T(8,128)(2,1)S(1)}, bf16[72,448]{1,0:T(8,128)(2,1)S(1)}) custom-call(bf16[72,2432]{1,0:T(8,128)(2,1)S(1)} %collective-permute-done.20.refs_0_, bf16[72,2432]{1,0:T(8,128)(2,1)S(1)} %collective-permute-done.21.refs_1_, bf16[448,2432]{1,0:T(8,128)(2,1)S(1)} %bitcast.76, bf16[448,2432]{1,0:T(8,128)(2,1)S(1)} %bitcast.82), custom_call_target="tpu_custom_call" | custom-call | flops 627572736 | bytes 4358144 | tf_op jit(solution)/shard_map/outward/pallas_call | solution.py:204
  106.7 2.0 %collective-permute-done.22.refs_0_ = bf16[72,2432]{1,0:T(8,128)(2,1)S(1)} collective-permute-done((bf16[72,2432]{1,0:T(8,128)(2,1)S(1)}, bf16[72,2432]{1,0:T(8,128)(2,1)S(1)}, u32[]{:S(2)}, u32[]{:S(2)}) %collective-permute-start.22) | collective-permute-done | bytes 350240 | tf_op jit(solution)/shard_map/ppermute | solution.py:300
  109.7 1.8 collective-permute-start.25
  111.4 1.5 collective-permute-start.26
  112.9 2.7 %outward.7 = (bf16[72,448]{1,0:T(8,128)(2,1)S(1)}, bf16[72,448]{1,0:T(8,128)(2,1)S(1)}) custom-call(bf16[72,2432]{1,0:T(8,128)(2,1)S(1)} %collective-permute-done.22.refs_0_, bf16[72,2432]{1,0:T(8,128)(2,1)S(1)} %collective-permute-done.23.refs_1_, bf16[448,2432]{1,0:T(8,128)(2,1)S(1)} %bitcast.77, bf16[448,2432]{1,0:T(8,128)(2,1)S(1)} %bitcast.83), custom_call_target="tpu_custom_call" | custom-call | flops 627572736 | bytes 4358144 | tf_op jit(solution)/shard_map/outward/pallas_call | solution.py:204
  115.6 5.1 %collective-permute-done.26.refs_1_ = bf16[72,448]{1,0:T(8,128)(2,1)S(1)} collective-permute-done((bf16[72,448]{1,0:T(8,128)(2,1)S(1)}, bf16[72,448]{1,0:T(8,128)(2,1)S(1)}, u32[]{:S(2)}, u32[]{:S(2)}) %collective-permute-start.26) | collective-permute-done | bytes 64544 | tf_op jit(solution)/shard_map/ppermute | solution.py:300
  120.9 2.6 %collective-permute-start.29 = (bf16[40,2432]{1,0:T(8,128)(2,1)S(1)}, bf16[40,2432]{1,0:T(8,128)(2,1)S(1)}, u32[]{:S(2)}, u32[]{:S(2)}) collective-permute-start(bf16[40,2432]{1,0:T(8,128)(2,1)S(1)} %slice.103), channel_id=1, source_target_pairs={{0,14},{1,15},{2,0},{3,1},{4,2},{5,3},{6,4},{7,5},{8,6},{9,7},{10,... | collective-permute-start | bytes 583688 | tf_op jit(solution)/shard_map/ppermute | solution.py:300
  123.6 1.4 collective-permute-start.30
  125.0 1.1 collective-permute-start.31
  126.1 2.7 %outward.8 = (bf16[72,448]{1,0:T(8,128)(2,1)S(1)}, bf16[72,448]{1,0:T(8,128)(2,1)S(1)}) custom-call(bf16[72,2432]{1,0:T(8,128)(2,1)S(1)} %collective-permute-done.24.refs_0_, bf16[72,2432]{1,0:T(8,128)(2,1)S(1)} %collective-permute-done.25.refs_1_, bf16[448,2432]{1,0:T(8,128)(2,1)S(1)} %bitcast.78, bf16[448,2432]{1,0:T(8,128)(2,1)S(1)} %bitcast.84), custom_call_target="tpu_custom_call" | custom-call | flops 627572736 | bytes 4358144 | tf_op jit(solution)/shard_map/outward/pallas_call | solution.py:204
  128.8 2.4 %collective-permute-start.32 = (bf16[72,448]{1,0:T(8,128)(2,1)S(1)}, bf16[72,448]{1,0:T(8,128)(2,1)S(1)}, u32[]{:S(2)}, u32[]{:S(2)}) collective-permute-start(bf16[72,448]{1,0:T(8,128)(2,1)S(1)} %get-tuple-element.77), channel_id=1, source_target_pairs={{0,10},{1,11},{2,12},{3,13},{4,14},{5,15},{6,0},{7,1},{8,2},{9,3},... | collective-permute-start | bytes 193544 | tf_op jit(solution)/shard_map/ppermute | solution.py:300
  131.2 1.0 collective-permute-start.34
  132.2 1.3 outward.9
  133.5 3.8 %collective-permute-start.33 = (bf16[72,448]{1,0:T(8,128)(2,1)S(1)}, bf16[72,448]{1,0:T(8,128)(2,1)S(1)}, u32[]{:S(2)}, u32[]{:S(2)}) collective-permute-start(bf16[72,448]{1,0:T(8,128)(2,1)S(1)} %outward.9), channel_id=1, source_target_pairs={{0,8},{1,9},{2,10},{3,11},{4,12},{5,13},{6,14},{7,15},{8,0},{9,1},... | collective-permute-start | bytes 193544 | tf_op jit(solution)/shard_map/ppermute | solution.py:300
  137.3 1.3 collective-permute-done.34.refs_5_
  138.6 3.7 %collective-permute-done.33.refs_4_ = bf16[72,448]{1,0:T(8,128)(2,1)S(1)} collective-permute-done((bf16[72,448]{1,0:T(8,128)(2,1)S(1)}, bf16[72,448]{1,0:T(8,128)(2,1)S(1)}, u32[]{:S(2)}, u32[]{:S(2)}) %collective-permute-start.33) | collective-permute-done | bytes 64544 | tf_op jit(solution)/shard_map/ppermute | solution.py:300
  142.4 1.0 settle.1
  143.4 27.0 %collective-permute-start.35 = (bf16[8,24,448]{2,1,0:T(8,128)(2,1)S(1)}, bf16[8,24,448]{2,1,0:T(8,128)(2,1)S(1)}, u32[]{:S(2)}, u32[]{:S(2)}) collective-permute-start(bf16[8,24,448]{2,1,0:T(8,128)(2,1)S(1)} %get-tuple-element.84), channel_id=1, source_target_pairs={{0,240},{1,241},{2,242},{3,243},{4,244},{5,245},{6,246},{7,247},{8... | collective-permute-start | bytes 516104 | tf_op jit(solution)/shard_map/ppermute | solution.py:314
  170.4 4.9 %collective-permute-start.37 = (bf16[8,24,448]{2,1,0:T(8,128)(2,1)S(1)}, bf16[8,24,448]{2,1,0:T(8,128)(2,1)S(1)}, u32[]{:S(2)}, u32[]{:S(2)}) collective-permute-start(bf16[8,24,448]{2,1,0:T(8,128)(2,1)S(1)} %get-tuple-element.86), channel_id=1, source_target_pairs={{0,16},{1,17},{2,18},{3,19},{4,20},{5,21},{6,22},{7,23},{8,24},{9,... | collective-permute-start | bytes 516104 | tf_op jit(solution)/shard_map/ppermute | solution.py:314
  175.3 3.5 %collective-permute-done.36.far_other = bf16[8,24,448]{2,1,0:T(8,128)(2,1)S(1)} collective-permute-done((bf16[8,24,448]{2,1,0:T(8,128)(2,1)S(1)}, bf16[8,24,448]{2,1,0:T(8,128)(2,1)S(1)}, u32[]{:S(2)}, u32[]{:S(2)}) %collective-permute-start.36) | collective-permute-done | bytes 172064 | tf_op jit(solution)/shard_map/ppermute | solution.py:314
  178.8 3.0 %collective-permute-done.38.near_other = bf16[8,24,448]{2,1,0:T(8,128)(2,1)S(1)} collective-permute-done((bf16[8,24,448]{2,1,0:T(8,128)(2,1)S(1)}, bf16[8,24,448]{2,1,0:T(8,128)(2,1)S(1)}, u32[]{:S(2)}, u32[]{:S(2)}) %collective-permute-start.38) | collective-permute-done | bytes 172064 | tf_op jit(solution)/shard_map/ppermute | solution.py:314
  181.8 5.0 %patch.1 = (bf16[128,7168]{1,0:T(8,128)(2,1)}, bf16[128,7168]{1,0:T(8,128)(2,1)}) custom-call(s32[3]{0:T(128)S(1)} %pad_add_fusion.place, bf16[128,7168]{1,0:T(8,128)(2,1)} %collective-permute-done.fraw, bf16[128,7168]{1,0:T(8,128)(2,1)} %collective-permute-done.1.braw, bf16[8,24,448]{2,1,0:T(8,128)(2,1)S(1)} %collective-permute-done.35.far, ...), custom_call_target="tpu_custom_call" | custom-call | tf_op jit(solution)/shard_map/patch/pallas_call | solution.py:287
  (78 shorter events, 7.8 us)
Async XLA Ops:
  0.6 37.2 %copy-start = (bf16[1,448,2432]{2,1,0:T(8,128)(2,1)S(1)}, bf16[1,448,2432]{2,1,0:T(8,128)(2,1)}, u32[]{:S(2)}) copy-start(bf16[1,448,2432]{2,1,0:T(8,128)(2,1)} %param.16) | copy-start | bytes 6537220
  6.5 38.0 %collective-permute-start = (bf16[128,7168]{1,0:T(8,128)(2,1)}, bf16[128,7168]{1,0:T(8,128)(2,1)}, u32[]{:S(2)}, u32[]{:S(2)}) collective-permute-start(bf16[128,7168]{1,0:T(8,128)(2,1)} %bitcast.88), channel_id=1, source_target_pairs={{0,16},{1,17},{2,18},{3,19},{4,20},{5,21},{6,22},{7,23},{8,24},{9,... | collective-permute-start | bytes 5505032 | tf_op jit(solution)/shard_map/ppermute | solution.py:314
  9.3 35.2 %collective-permute-start.1 = (bf16[128,7168]{1,0:T(8,128)(2,1)}, bf16[128,7168]{1,0:T(8,128)(2,1)}, u32[]{:S(2)}, u32[]{:S(2)}) collective-permute-start(bf16[128,7168]{1,0:T(8,128)(2,1)} %bitcast.90), channel_id=1, source_target_pairs={{0,240},{1,241},{2,242},{3,243},{4,244},{5,245},{6,246},{7,247},{8... | collective-permute-start | bytes 5505032 | tf_op jit(solution)/shard_map/ppermute | solution.py:314
  10.0 27.8 %all-to-all-start = ((bf16[16,56,448]{2,1,0:T(8,128)(2,1)}), bf16[16,56,448]{2,1,0:T(8,128)(2,1)S(1)}, u32[]{:S(2)}, u32[]{:S(2)}) async-start(bf16[16,56,448]{2,1,0:T(8,128)(2,1)} %get-tuple-element.47), calls=%async_computation | async-start | bytes 1835008 | tf_op jit(solution)/shard_map/all_to_all | solution.py:392
  37.8 1.6 copy-start.1
  44.6 5.5 %collective-permute-start.11 = (bf16[48,1152]{1,0:T(8,128)(2,1)S(1)}, bf16[48,1152]{1,0:T(8,128)(2,1)S(1)}, u32[]{:S(2)}, u32[]{:S(2)}) collective-permute-start(bf16[48,1152]{1,0:T(8,128)(2,1)S(1)} %get-tuple-element.63), channel_id=1, source_target_pairs={{0,2},{1,3},{2,4},{3,5},{4,6},{5,7},{6,8},{7,9},{8,10},{9,11},{10,... | collective-permute-start | bytes 331784 | tf_op jit(solution)/shard_map/ppermute | solution.py:300
  44.8 7.7 %collective-permute-start.15 = (bf16[56,1152]{1,0:T(8,128)(2,1)S(1)}, bf16[56,1152]{1,0:T(8,128)(2,1)S(1)}, u32[]{:S(2)}, u32[]{:S(2)}) collective-permute-start(bf16[56,1152]{1,0:T(8,128)(2,1)S(1)} %get-tuple-element.64), channel_id=1, source_target_pairs={{0,14},{1,15},{2,0},{3,1},{4,2},{5,3},{6,4},{7,5},{8,6},{9,7},{10,... | collective-permute-start | bytes 387080 | tf_op jit(solution)/shard_map/ppermute | solution.py:300
  47.5 4.9 %collective-permute-start.2 = (bf16[48,1280]{1,0:T(8,128)(2,1)S(1)}, bf16[48,1280]{1,0:T(8,128)(2,1)S(1)}, u32[]{:S(2)}, u32[]{:S(2)}) collective-permute-start(bf16[48,1280]{1,0:T(8,128)(2,1)S(1)} %get-tuple-element.60), channel_id=1, source_target_pairs={{0,2},{1,3},{2,4},{3,5},{4,6},{5,7},{6,8},{7,9},{8,10},{9,11},{10,... | collective-permute-start | bytes 368648 | tf_op jit(solution)/shard_map/ppermute | solution.py:300
  47.5 7.9 %collective-permute-start.6 = (bf16[56,1280]{1,0:T(8,128)(2,1)S(1)}, bf16[56,1280]{1,0:T(8,128)(2,1)S(1)}, u32[]{:S(2)}, u32[]{:S(2)}) collective-permute-start(bf16[56,1280]{1,0:T(8,128)(2,1)S(1)} %get-tuple-element.61), channel_id=1, source_target_pairs={{0,14},{1,15},{2,0},{3,1},{4,2},{5,3},{6,4},{7,5},{8,6},{9,7},{10,... | collective-permute-start | bytes 430088 | tf_op jit(solution)/shard_map/ppermute | solution.py:300
  50.2 6.3 %collective-permute-start.12 = (bf16[104,1152]{1,0:T(8,128)(2,1)S(1)}, bf16[104,1152]{1,0:T(8,128)(2,1)S(1)}, u32[]{:S(2)}, u32[]{:S(2)}) collective-permute-start(bf16[104,1152]{1,0:T(8,128)(2,1)S(1)} %pad_maximum_fusion.3), channel_id=1, source_target_pairs={{0,2},{1,3},{2,4},{3,5},{4,6},{5,7},{6,8},{7,9},{8,10},{9,11},{10,... | collective-permute-start | bytes 718856 | tf_op jit(solution)/shard_map/ppermute | solution.py:300
  52.5 6.9 %collective-permute-start.3 = (bf16[104,1280]{1,0:T(8,128)(2,1)S(1)}, bf16[104,1280]{1,0:T(8,128)(2,1)S(1)}, u32[]{:S(2)}, u32[]{:S(2)}) collective-permute-start(bf16[104,1280]{1,0:T(8,128)(2,1)S(1)} %pad_maximum_fusion.1), channel_id=1, source_target_pairs={{0,2},{1,3},{2,4},{3,5},{4,6},{5,7},{6,8},{7,9},{8,10},{9,11},{10,... | collective-permute-start | bytes 798728 | tf_op jit(solution)/shard_map/ppermute | solution.py:300
  52.6 6.9 %collective-permute-start.16 = (bf16[104,1152]{1,0:T(8,128)(2,1)S(1)}, bf16[104,1152]{1,0:T(8,128)(2,1)S(1)}, u32[]{:S(2)}, u32[]{:S(2)}) collective-permute-start(bf16[104,1152]{1,0:T(8,128)(2,1)S(1)} %pad_maximum_fusion.4), channel_id=1, source_target_pairs={{0,14},{1,15},{2,0},{3,1},{4,2},{5,3},{6,4},{7,5},{8,6},{9,7},{10,... | collective-permute-start | bytes 718856 | tf_op jit(solution)/shard_map/ppermute | solution.py:300
  55.4 10.5 %collective-permute-start.7 = (bf16[104,1280]{1,0:T(8,128)(2,1)S(1)}, bf16[104,1280]{1,0:T(8,128)(2,1)S(1)}, u32[]{:S(2)}, u32[]{:S(2)}) collective-permute-start(bf16[104,1280]{1,0:T(8,128)(2,1)S(1)} %pad_maximum_fusion.2), channel_id=1, source_target_pairs={{0,14},{1,15},{2,0},{3,1},{4,2},{5,3},{6,4},{7,5},{8,6},{9,7},{10,... | collective-permute-start | bytes 798728 | tf_op jit(solution)/shard_map/ppermute | solution.py:300
  56.5 7.7 %collective-permute-start.13 = (bf16[104,1152]{1,0:T(8,128)(2,1)S(1)}, bf16[104,1152]{1,0:T(8,128)(2,1)S(1)}, u32[]{:S(2)}, u32[]{:S(2)}) collective-permute-start(bf16[104,1152]{1,0:T(8,128)(2,1)S(1)} %fusion.8), channel_id=1, source_target_pairs={{0,2},{1,3},{2,4},{3,5},{4,6},{5,7},{6,8},{7,9},{8,10},{9,11},{10,... | collective-permute-start | bytes 718856 | tf_op jit(solution)/shard_map/ppermute | solution.py:300
  59.4 9.5 %collective-permute-start.4 = (bf16[104,1280]{1,0:T(8,128)(2,1)S(1)}, bf16[104,1280]{1,0:T(8,128)(2,1)S(1)}, u32[]{:S(2)}, u32[]{:S(2)}) collective-permute-start(bf16[104,1280]{1,0:T(8,128)(2,1)S(1)} %fusion.2), channel_id=1, source_target_pairs={{0,2},{1,3},{2,4},{3,5},{4,6},{5,7},{6,8},{7,9},{8,10},{9,11},{10,... | collective-permute-start | bytes 798728 | tf_op jit(solution)/shard_map/ppermute | solution.py:300
  64.4 6.2 %collective-permute-start.17 = (bf16[104,1152]{1,0:T(8,128)(2,1)S(1)}, bf16[104,1152]{1,0:T(8,128)(2,1)S(1)}, u32[]{:S(2)}, u32[]{:S(2)}) collective-permute-start(bf16[104,1152]{1,0:T(8,128)(2,1)S(1)} %get-tuple-element.93), channel_id=1, source_target_pairs={{0,14},{1,15},{2,0},{3,1},{4,2},{5,3},{6,4},{7,5},{8,6},{9,7},{10,... | collective-permute-start | bytes 718856 | tf_op jit(solution)/shard_map/ppermute | solution.py:300
  64.5 13.3 %collective-permute-start.14 = (bf16[104,1152]{1,0:T(8,128)(2,1)S(1)}, bf16[104,1152]{1,0:T(8,128)(2,1)S(1)}, u32[]{:S(2)}, u32[]{:S(2)}) collective-permute-start(bf16[104,1152]{1,0:T(8,128)(2,1)S(1)} %get-tuple-element.92), channel_id=1, source_target_pairs={{0,2},{1,3},{2,4},{3,5},{4,6},{5,7},{6,8},{7,9},{8,10},{9,11},{10,... | collective-permute-start | bytes 718856 | tf_op jit(solution)/shard_map/ppermute | solution.py:300
  69.1 8.4 %collective-permute-start.8 = (bf16[104,1280]{1,0:T(8,128)(2,1)S(1)}, bf16[104,1280]{1,0:T(8,128)(2,1)S(1)}, u32[]{:S(2)}, u32[]{:S(2)}) collective-permute-start(bf16[104,1280]{1,0:T(8,128)(2,1)S(1)} %get-tuple-element.91), channel_id=1, source_target_pairs={{0,14},{1,15},{2,0},{3,1},{4,2},{5,3},{6,4},{7,5},{8,6},{9,7},{10,... | collective-permute-start | bytes 798728 | tf_op jit(solution)/shard_map/ppermute | solution.py:300
  69.2 12.2 %collective-permute-start.5 = (bf16[104,1280]{1,0:T(8,128)(2,1)S(1)}, bf16[104,1280]{1,0:T(8,128)(2,1)S(1)}, u32[]{:S(2)}, u32[]{:S(2)}) collective-permute-start(bf16[104,1280]{1,0:T(8,128)(2,1)S(1)} %get-tuple-element.90), channel_id=1, source_target_pairs={{0,2},{1,3},{2,4},{3,5},{4,6},{5,7},{6,8},{7,9},{8,10},{9,11},{10,... | collective-permute-start | bytes 798728 | tf_op jit(solution)/shard_map/ppermute | solution.py:300
  70.7 10.2 %collective-permute-start.18 = (bf16[104,1152]{1,0:T(8,128)(2,1)S(1)}, bf16[104,1152]{1,0:T(8,128)(2,1)S(1)}, u32[]{:S(2)}, u32[]{:S(2)}) collective-permute-start(bf16[104,1152]{1,0:T(8,128)(2,1)S(1)} %fusion.7), channel_id=1, source_target_pairs={{0,14},{1,15},{2,0},{3,1},{4,2},{5,3},{6,4},{7,5},{8,6},{9,7},{10,... | collective-permute-start | bytes 718856 | tf_op jit(solution)/shard_map/ppermute | solution.py:300
  77.6 6.2 %collective-permute-start.9 = (bf16[104,1280]{1,0:T(8,128)(2,1)S(1)}, bf16[104,1280]{1,0:T(8,128)(2,1)S(1)}, u32[]{:S(2)}, u32[]{:S(2)}) collective-permute-start(bf16[104,1280]{1,0:T(8,128)(2,1)S(1)} %fusion.1), channel_id=1, source_target_pairs={{0,14},{1,15},{2,0},{3,1},{4,2},{5,3},{6,4},{7,5},{8,6},{9,7},{10,... | collective-permute-start | bytes 798728 | tf_op jit(solution)/shard_map/ppermute | solution.py:300
  81.0 5.4 %collective-permute-start.19 = (bf16[104,1152]{1,0:T(8,128)(2,1)S(1)}, bf16[104,1152]{1,0:T(8,128)(2,1)S(1)}, u32[]{:S(2)}, u32[]{:S(2)}) collective-permute-start(bf16[104,1152]{1,0:T(8,128)(2,1)S(1)} %fusion.11), channel_id=1, source_target_pairs={{0,1},{1,0},{2,3},{3,2},{4,5},{5,4},{6,7},{7,6},{8,9},{9,8},{10,11... | collective-permute-start | bytes 718856 | tf_op jit(solution)/shard_map/ppermute | solution.py:304
  83.9 5.4 %collective-permute-start.10 = (bf16[104,1280]{1,0:T(8,128)(2,1)S(1)}, bf16[104,1280]{1,0:T(8,128)(2,1)S(1)}, u32[]{:S(2)}, u32[]{:S(2)}) collective-permute-start(bf16[104,1280]{1,0:T(8,128)(2,1)S(1)} %fusion.5), channel_id=1, source_target_pairs={{0,1},{1,0},{2,3},{3,2},{4,5},{5,4},{6,7},{7,6},{8,9},{9,8},{10,11... | collective-permute-start | bytes 798728 | tf_op jit(solution)/shard_map/ppermute | solution.py:304
  89.6 8.2 %collective-permute-start.20 = (bf16[72,2432]{1,0:T(8,128)(2,1)S(1)}, bf16[72,2432]{1,0:T(8,128)(2,1)S(1)}, u32[]{:S(2)}, u32[]{:S(2)}) collective-permute-start(bf16[72,2432]{1,0:T(8,128)(2,1)S(1)} %maximum_maximum_fusion.refs_0_), channel_id=1, source_target_pairs={{0,2},{1,3},{2,4},{3,5},{4,6},{5,7},{6,8},{7,9},{8,10},{9,11},{10,... | collective-permute-start | bytes 1050632 | tf_op jit(solution)/shard_map/ppermute | solution.py:300
  90.4 11.0 %collective-permute-start.21 = (bf16[72,2432]{1,0:T(8,128)(2,1)S(1)}, bf16[72,2432]{1,0:T(8,128)(2,1)S(1)}, u32[]{:S(2)}, u32[]{:S(2)}) collective-permute-start(bf16[72,2432]{1,0:T(8,128)(2,1)S(1)} %maximum_maximum_fusion.refs_0_), channel_id=1, source_target_pairs={{0,14},{1,15},{2,0},{3,1},{4,2},{5,3},{6,4},{7,5},{8,6},{9,7},{10,... | collective-permute-start | bytes 1050632 | tf_op jit(solution)/shard_map/ppermute | solution.py:300
  101.4 7.4 %collective-permute-start.22 = (bf16[72,2432]{1,0:T(8,128)(2,1)S(1)}, bf16[72,2432]{1,0:T(8,128)(2,1)S(1)}, u32[]{:S(2)}, u32[]{:S(2)}) collective-permute-start(bf16[72,2432]{1,0:T(8,128)(2,1)S(1)} %collective-permute-done.20.refs_0_), channel_id=1, source_target_pairs={{0,2},{1,3},{2,4},{3,5},{4,6},{5,7},{6,8},{7,9},{8,10},{9,11},{10,... | collective-permute-start | bytes 1050632 | tf_op jit(solution)/shard_map/ppermute | solution.py:300
  101.8 7.0 %collective-permute-start.23 = (bf16[72,2432]{1,0:T(8,128)(2,1)S(1)}, bf16[72,2432]{1,0:T(8,128)(2,1)S(1)}, u32[]{:S(2)}, u32[]{:S(2)}) collective-permute-start(bf16[72,2432]{1,0:T(8,128)(2,1)S(1)} %collective-permute-done.21.refs_1_), channel_id=1, source_target_pairs={{0,14},{1,15},{2,0},{3,1},{4,2},{5,3},{6,4},{7,5},{8,6},{9,7},{10,... | collective-permute-start | bytes 1050632 | tf_op jit(solution)/shard_map/ppermute | solution.py:300
  108.8 12.1 %collective-permute-start.24 = (bf16[72,2432]{1,0:T(8,128)(2,1)S(1)}, bf16[72,2432]{1,0:T(8,128)(2,1)S(1)}, u32[]{:S(2)}, u32[]{:S(2)}) collective-permute-start(bf16[72,2432]{1,0:T(8,128)(2,1)S(1)} %collective-permute-done.22.refs_0_), channel_id=1, source_target_pairs={{0,2},{1,3},{2,4},{3,5},{4,6},{5,7},{6,8},{7,9},{8,10},{9,11},{10,... | collective-permute-start | bytes 1050632 | tf_op jit(solution)/shard_map/ppermute | solution.py:300
  109.7 11.2 %collective-permute-start.25 = (bf16[72,2432]{1,0:T(8,128)(2,1)S(1)}, bf16[72,2432]{1,0:T(8,128)(2,1)S(1)}, u32[]{:S(2)}, u32[]{:S(2)}) collective-permute-start(bf16[72,2432]{1,0:T(8,128)(2,1)S(1)} %collective-permute-done.23.refs_1_), channel_id=1, source_target_pairs={{0,14},{1,15},{2,0},{3,1},{4,2},{5,3},{6,4},{7,5},{8,6},{9,7},{10,... | collective-permute-start | bytes 1050632 | tf_op jit(solution)/shard_map/ppermute | solution.py:300
  111.4 9.2 %collective-permute-start.26 = (bf16[72,448]{1,0:T(8,128)(2,1)S(1)}, bf16[72,448]{1,0:T(8,128)(2,1)S(1)}, u32[]{:S(2)}, u32[]{:S(2)}) collective-permute-start(bf16[72,448]{1,0:T(8,128)(2,1)S(1)} %get-tuple-element.68), channel_id=1, source_target_pairs={{0,14},{1,15},{2,0},{3,1},{4,2},{5,3},{6,4},{7,5},{8,6},{9,7},{10,... | collective-permute-start | bytes 193544 | tf_op jit(solution)/shard_map/ppermute | solution.py:300
  112.9 8.0 %collective-permute-start.27 = (bf16[72,448]{1,0:T(8,128)(2,1)S(1)}, bf16[72,448]{1,0:T(8,128)(2,1)S(1)}, u32[]{:S(2)}, u32[]{:S(2)}) collective-permute-start(bf16[72,448]{1,0:T(8,128)(2,1)S(1)} %get-tuple-element.69), channel_id=1, source_target_pairs={{0,2},{1,3},{2,4},{3,5},{4,6},{5,7},{6,8},{7,9},{8,10},{9,11},{10,... | collective-permute-start | bytes 193544 | tf_op jit(solution)/shard_map/ppermute | solution.py:300
  120.9 11.2 %collective-permute-start.29 = (bf16[40,2432]{1,0:T(8,128)(2,1)S(1)}, bf16[40,2432]{1,0:T(8,128)(2,1)S(1)}, u32[]{:S(2)}, u32[]{:S(2)}) collective-permute-start(bf16[40,2432]{1,0:T(8,128)(2,1)S(1)} %slice.103), channel_id=1, source_target_pairs={{0,14},{1,15},{2,0},{3,1},{4,2},{5,3},{6,4},{7,5},{8,6},{9,7},{10,... | collective-permute-start | bytes 583688 | tf_op jit(solution)/shard_map/ppermute | solution.py:300
  123.5 8.6 %collective-permute-start.28 = (bf16[32,2432]{1,0:T(8,128)(2,1)S(1)}, bf16[32,2432]{1,0:T(8,128)(2,1)S(1)}, u32[]{:S(2)}, u32[]{:S(2)}) collective-permute-start(bf16[32,2432]{1,0:T(8,128)(2,1)S(1)} %slice.102), channel_id=1, source_target_pairs={{0,2},{1,3},{2,4},{3,5},{4,6},{5,7},{6,8},{7,9},{8,10},{9,11},{10,... | collective-permute-start | bytes 466952 | tf_op jit(solution)/shard_map/ppermute | solution.py:300
  123.6 7.5 %collective-permute-start.30 = (bf16[72,448]{1,0:T(8,128)(2,1)S(1)}, bf16[72,448]{1,0:T(8,128)(2,1)S(1)}, u32[]{:S(2)}, u32[]{:S(2)}) collective-permute-start(bf16[72,448]{1,0:T(8,128)(2,1)S(1)} %get-tuple-element.72), channel_id=1, source_target_pairs={{0,12},{1,13},{2,14},{3,15},{4,0},{5,1},{6,2},{7,3},{8,4},{9,5},{1... | collective-permute-start | bytes 193544 | tf_op jit(solution)/shard_map/ppermute | solution.py:300
  125.0 7.1 %collective-permute-start.31 = (bf16[72,448]{1,0:T(8,128)(2,1)S(1)}, bf16[72,448]{1,0:T(8,128)(2,1)S(1)}, u32[]{:S(2)}, u32[]{:S(2)}) collective-permute-start(bf16[72,448]{1,0:T(8,128)(2,1)S(1)} %get-tuple-element.73), channel_id=1, source_target_pairs={{0,4},{1,5},{2,6},{3,7},{4,8},{5,9},{6,10},{7,11},{8,12},{9,13},{1... | collective-permute-start | bytes 193544 | tf_op jit(solution)/shard_map/ppermute | solution.py:300
  128.8 8.6 %collective-permute-start.32 = (bf16[72,448]{1,0:T(8,128)(2,1)S(1)}, bf16[72,448]{1,0:T(8,128)(2,1)S(1)}, u32[]{:S(2)}, u32[]{:S(2)}) collective-permute-start(bf16[72,448]{1,0:T(8,128)(2,1)S(1)} %get-tuple-element.77), channel_id=1, source_target_pairs={{0,10},{1,11},{2,12},{3,13},{4,14},{5,15},{6,0},{7,1},{8,2},{9,3},... | collective-permute-start | bytes 193544 | tf_op jit(solution)/shard_map/ppermute | solution.py:300
  131.2 7.5 %collective-permute-start.34 = (bf16[72,448]{1,0:T(8,128)(2,1)S(1)}, bf16[72,448]{1,0:T(8,128)(2,1)S(1)}, u32[]{:S(2)}, u32[]{:S(2)}) collective-permute-start(bf16[72,448]{1,0:T(8,128)(2,1)S(1)} %get-tuple-element.78), channel_id=1, source_target_pairs={{0,6},{1,7},{2,8},{3,9},{4,10},{5,11},{6,12},{7,13},{8,14},{9,15},... | collective-permute-start | bytes 193544 | tf_op jit(solution)/shard_map/ppermute | solution.py:300
  132.2 10.2 %copy-start.2 = (f32[8,128]{1,0:T(8,128)S(1)}, f32[8,128]{1,0:T(8,128)}, u32[]{:S(2)}) copy-start(f32[8,128]{1,0:T(8,128)} %get-tuple-element.58.meta) | copy-start | bytes 12292
  133.5 8.9 %collective-permute-start.33 = (bf16[72,448]{1,0:T(8,128)(2,1)S(1)}, bf16[72,448]{1,0:T(8,128)(2,1)S(1)}, u32[]{:S(2)}, u32[]{:S(2)}) collective-permute-start(bf16[72,448]{1,0:T(8,128)(2,1)S(1)} %outward.9), channel_id=1, source_target_pairs={{0,8},{1,9},{2,10},{3,11},{4,12},{5,13},{6,14},{7,15},{8,0},{9,1},... | collective-permute-start | bytes 193544 | tf_op jit(solution)/shard_map/ppermute | solution.py:300
  143.4 31.8 %collective-permute-start.35 = (bf16[8,24,448]{2,1,0:T(8,128)(2,1)S(1)}, bf16[8,24,448]{2,1,0:T(8,128)(2,1)S(1)}, u32[]{:S(2)}, u32[]{:S(2)}) collective-permute-start(bf16[8,24,448]{2,1,0:T(8,128)(2,1)S(1)} %get-tuple-element.84), channel_id=1, source_target_pairs={{0,240},{1,241},{2,242},{3,243},{4,244},{5,245},{6,246},{7,247},{8... | collective-permute-start | bytes 516104 | tf_op jit(solution)/shard_map/ppermute | solution.py:314
  170.4 8.4 %collective-permute-start.36 = (bf16[8,24,448]{2,1,0:T(8,128)(2,1)S(1)}, bf16[8,24,448]{2,1,0:T(8,128)(2,1)S(1)}, u32[]{:S(2)}, u32[]{:S(2)}) collective-permute-start(bf16[8,24,448]{2,1,0:T(8,128)(2,1)S(1)} %get-tuple-element.85), channel_id=1, source_target_pairs={{0,241},{1,240},{2,243},{3,242},{4,245},{5,244},{6,247},{7,246},{8... | collective-permute-start | bytes 516104 | tf_op jit(solution)/shard_map/ppermute | solution.py:314
  170.4 8.4 %collective-permute-start.37 = (bf16[8,24,448]{2,1,0:T(8,128)(2,1)S(1)}, bf16[8,24,448]{2,1,0:T(8,128)(2,1)S(1)}, u32[]{:S(2)}, u32[]{:S(2)}) collective-permute-start(bf16[8,24,448]{2,1,0:T(8,128)(2,1)S(1)} %get-tuple-element.86), channel_id=1, source_target_pairs={{0,16},{1,17},{2,18},{3,19},{4,20},{5,21},{6,22},{7,23},{8,24},{9,... | collective-permute-start | bytes 516104 | tf_op jit(solution)/shard_map/ppermute | solution.py:314
  175.2 6.5 %collective-permute-start.38 = (bf16[8,24,448]{2,1,0:T(8,128)(2,1)S(1)}, bf16[8,24,448]{2,1,0:T(8,128)(2,1)S(1)}, u32[]{:S(2)}, u32[]{:S(2)}) collective-permute-start(bf16[8,24,448]{2,1,0:T(8,128)(2,1)S(1)} %get-tuple-element.87), channel_id=1, source_target_pairs={{0,17},{1,16},{2,19},{3,18},{4,21},{5,20},{6,23},{7,22},{8,25},{9,... | collective-permute-start | bytes 516104 | tf_op jit(solution)/shard_map/ppermute | solution.py:314

commit v2 on v1

--- a/solution.py
+++ b/solution.py
@@ -61,16 +61,13 @@
 def pick_kernel(froutes, fgates, broutes, bgates, acts, saved, cot, packed, meta, held, sems):
     sources = (acts, saved, cot)
 
-    def strip(j):
-        return pl.ds(pl.multiple_of(j * WIDE, TOK), WIDE)
+    strips = 4
 
     def fetch(j, i):
-        return pltpu.make_async_copy(
-            sources[i].at[:, strip(j)], held.at[i, :, strip(j)], sems.at[j, i]
-        )
-
-    @pl.loop(0, NODES)
-    def _(j):
+        cols = pl.ds(pl.multiple_of(j * (D // strips), TOK), D // strips)
+        return pltpu.make_async_copy(sources[i].at[:, cols], held.at[i, :, cols], sems.at[j, i])
+
+    for j in range(strips):
         for i in range(3):
             fetch(j, i).start()
 
@@ -93,14 +90,17 @@
         rows = jnp.where(line == at, value, rows)
     meta[...] = rows
 
-    @pl.loop(0, NODES)
+    @pl.loop(0, strips)
     def _(j):
         for i in range(3):
             fetch(j, i).wait()
-        x, saves, raw = (held[i, :, strip(j)] for i in range(3))
-        rows = (dot(px, x) + dot(ps, saves) + gate * dot(pu, raw)).astype(BF)
-        packed[2 * j] = rows[:, :COLS]
-        packed[2 * j + 1] = rows[:, COLS:]
+        for half in range(2):
+            k = 2 * j + half
+            cols = pl.ds(pl.multiple_of(k * WIDE, TOK), WIDE)
+            x, saves, raw = (held[i, :, cols] for i in range(3))
+            rows = (dot(px, x) + dot(ps, saves) + gate * dot(pu, raw)).astype(BF)
+            packed[2 * k] = rows[:, :COLS]
+            packed[2 * k + 1] = rows[:, COLS:]
 
 
 def pick(froutes, fgates, broutes, bgates, acts, saved, cot):
@@ -110,7 +110,7 @@
         pick_kernel,
         in_specs=[vmem] * 4 + [anywhere] * 3,
         out_specs=(vmem,) * 2,
-        scratch_shapes=[pltpu.VMEM((3, TOK, D), BF), pltpu.SemaphoreType.DMA((NODES, 3))],
+        scratch_shapes=[pltpu.VMEM((3, TOK, D), BF), pltpu.SemaphoreType.DMA((4, 3))],
         out_shape=(
             jax.ShapeDtypeStruct((2 * NODES, PICK, COLS), BF),
             jax.ShapeDtypeStruct((8, TOK), F32),

time: 187 us -> 186 us (level)
  transfers between devices with their start and end apart: 40 -> 40, of which waited for: 20 -> 19; matrix products, arithmetic and copies ran while one was open for 1% -> 1% of each run, Pallas kernels for 8% -> 9%
where the time goes in v2:
time: 186 us
  starting transfers between devices  80.8 us (43%)
  waiting for transfers between devices  74.1 us (40%)
  Pallas kernels  26.9 us (14%)
    ppermute x31, waiting for transfers between devices, around(): return lax.ppermute(value, 'expert', pairs)  43.3 us
    ppermute x31, starting transfers between devices, around(): return lax.ppermute(value, 'expert', pairs)  36.5 us
    ppermute x6, starting transfers between devices, section_move(): return lax.ppermute(value, ('section', 'expert'), pairs)  35 us
    all_to_all x1, waiting for transfers between devices, per_device(): lax.all_to_all(packed, 'expert', split_axis=0, concat_axis=0, tiled=True)  19.1 us
    pallas_call x5, Pallas kernels, outward(): pl.pallas_call(functools.partial(outward_kernel, count), out_shape=[jax.S...  10.7 us
    all_to_all x1, starting transfers between devices, per_device(): lax.all_to_all(packed, 'expert', split_axis=0, concat_axis=0, tiled=True)  8.57 us
    ppermute x6, waiting for transfers between devices, section_move(): return lax.ppermute(value, ('section', 'expert'), pairs)  6.52 us
    pallas_call x1, Pallas kernels, partial_sums(): pl.pallas_call(partial_kernel, out_shape=shapes, in_specs=[pl.BlockSpec(m...  5.16 us
  transfers between devices with their start and end apart: 40, of which 19 were waited for; matrix products, arithmetic and copies ran while one was open for 1% of the time, Pallas kernels for 9%

profile of v2, /device:TPU:1, one launch (start us, length us, event | category | flops | bytes accessed | tf_op | source)
XLA Modules:
  0.0 186.0 jit_solution(46535764125267562)
XLA Ops:
  0.6 5.0 %pick.1 = (bf16[16,56,448]{2,1,0:T(8,128)(2,1)}, f32[8,128]{1,0:T(8,128)}) custom-call(s32[2,128]{1,0:T(2,128)} %bitcast.91, f32[2,128]{1,0:T(2,128)} %bitcast.92, s32[2,128]{1,0:T(2,128)} %bitcast.93, f32[2,128]{1,0:T(2,128)} %bitcast.94, bf16[128,7168]{1,0:T(8,128)(2,1)} %bitcast.87, bf16[128,7168]{1,0:T(8,128)(2,1)} %bitcast.86, bf16[128,7168]{1,0:T(8,128)(2,1)} %bitcast.89), custom_call_target="tpu_custom_call" | custom-call | tf_op jit(solution)/shard_map/pick/pallas_call | solution.py:109
  5.6 2.8 %collective-permute-start = (bf16[128,7168]{1,0:T(8,128)(2,1)}, bf16[128,7168]{1,0:T(8,128)(2,1)}, u32[]{:S(2)}, u32[]{:S(2)}) collective-permute-start(bf16[128,7168]{1,0:T(8,128)(2,1)} %bitcast.88), channel_id=1, source_target_pairs={{0,16},{1,17},{2,18},{3,19},{4,20},{5,21},{6,22},{7,23},{8,24},{9,... | collective-permute-start | bytes 5505032 | tf_op jit(solution)/shard_map/ppermute | solution.py:314
  9.1 8.6 %all-to-all-start = ((bf16[16,56,448]{2,1,0:T(8,128)(2,1)}), bf16[16,56,448]{2,1,0:T(8,128)(2,1)S(1)}, u32[]{:S(2)}, u32[]{:S(2)}) async-start(bf16[16,56,448]{2,1,0:T(8,128)(2,1)} %get-tuple-element.47), calls=%async_computation | async-start | bytes 1835008 | tf_op jit(solution)/shard_map/all_to_all | solution.py:392
  17.7 19.1 %all-to-all-done.picks = bf16[16,56,448]{2,1,0:T(8,128)(2,1)S(1)} async-done(((bf16[16,56,448]{2,1,0:T(8,128)(2,1)}), bf16[16,56,448]{2,1,0:T(8,128)(2,1)S(1)}, u32[]{:S(2)}, u32[]{:S(2)}) %all-to-all-start) | async-done | bytes 802848 | tf_op jit(solution)/shard_map/all_to_all | solution.py:392
  36.9 1.6 copy-done.1
  38.5 5.2 %partials.1 = (bf16[48,1280]{1,0:T(8,128)(2,1)S(1)}, bf16[56,1280]{1,0:T(8,128)(2,1)S(1)}, bf16[48,1152]{1,0:T(8,128)(2,1)S(1)}, bf16[56,1152]{1,0:T(8,128)(2,1)...) custom-call(s32[3]{0:T(128)S(1)} %pad_add_fusion.place, ...), custom_call_target="tpu_custom_call" | custom-call | tf_op jit(solution)/shard_map/partials/pallas_call | solution.py:173
  44.0 2.6 %collective-permute-start.15 = (bf16[56,1152]{1,0:T(8,128)(2,1)S(1)}, bf16[56,1152]{1,0:T(8,128)(2,1)S(1)}, u32[]{:S(2)}, u32[]{:S(2)}) collective-permute-start(bf16[56,1152]{1,0:T(8,128)(2,1)S(1)} %get-tuple-element.64), channel_id=1, source_target_pairs={{0,14},{1,15},{2,0},{3,1},{4,2},{5,3},{6,4},{7,5},{8,6},{9,7},{10,... | collective-permute-start | bytes 387080 | tf_op jit(solution)/shard_map/ppermute | solution.py:300
  46.6 2.7 %collective-permute-start.6 = (bf16[56,1280]{1,0:T(8,128)(2,1)S(1)}, bf16[56,1280]{1,0:T(8,128)(2,1)S(1)}, u32[]{:S(2)}, u32[]{:S(2)}) collective-permute-start(bf16[56,1280]{1,0:T(8,128)(2,1)S(1)} %get-tuple-element.61), channel_id=1, source_target_pairs={{0,14},{1,15},{2,0},{3,1},{4,2},{5,3},{6,4},{7,5},{8,6},{9,7},{10,... | collective-permute-start | bytes 430088 | tf_op jit(solution)/shard_map/ppermute | solution.py:300
  49.4 2.1 %collective-permute-done.2 = bf16[48,1280]{1,0:T(8,128)(2,1)S(1)} collective-permute-done((bf16[48,1280]{1,0:T(8,128)(2,1)S(1)}, bf16[48,1280]{1,0:T(8,128)(2,1)S(1)}, u32[]{:S(2)}, u32[]{:S(2)}) %collective-permute-start.2) | collective-permute-done | bytes 122912 | tf_op jit(solution)/shard_map/ppermute | solution.py:300
  51.8 2.7 %collective-permute-start.16 = (bf16[104,1152]{1,0:T(8,128)(2,1)S(1)}, bf16[104,1152]{1,0:T(8,128)(2,1)S(1)}, u32[]{:S(2)}, u32[]{:S(2)}) collective-permute-start(bf16[104,1152]{1,0:T(8,128)(2,1)S(1)} %pad_maximum_fusion.4), channel_id=1, source_target_pairs={{0,14},{1,15},{2,0},{3,1},{4,2},{5,3},{6,4},{7,5},{8,6},{9,7},{10,... | collective-permute-start | bytes 718856 | tf_op jit(solution)/shard_map/ppermute | solution.py:300
  56.3 2.2 %collective-permute-done.3 = bf16[104,1280]{1,0:T(8,128)(2,1)S(1)} collective-permute-done((bf16[104,1280]{1,0:T(8,128)(2,1)S(1)}, bf16[104,1280]{1,0:T(8,128)(2,1)S(1)}, u32[]{:S(2)}, u32[]{:S(2)}) %collective-permute-start.3) | collective-permute-done | bytes 266272 | tf_op jit(solution)/shard_map/ppermute | solution.py:300
  58.6 4.6 %collective-permute-done.13 = bf16[104,1152]{1,0:T(8,128)(2,1)S(1)} collective-permute-done((bf16[104,1152]{1,0:T(8,128)(2,1)S(1)}, bf16[104,1152]{1,0:T(8,128)(2,1)S(1)}, u32[]{:S(2)}, u32[]{:S(2)}) %collective-permute-start.13) | collective-permute-done | bytes 239648 | tf_op jit(solution)/shard_map/ppermute | solution.py:300
  63.7 1.5 collective-permute-start.14
  65.1 2.9 %collective-permute-done.4 = bf16[104,1280]{1,0:T(8,128)(2,1)S(1)} collective-permute-done((bf16[104,1280]{1,0:T(8,128)(2,1)S(1)}, bf16[104,1280]{1,0:T(8,128)(2,1)S(1)}, u32[]{:S(2)}, u32[]{:S(2)}) %collective-permute-start.4) | collective-permute-done | bytes 266272 | tf_op jit(solution)/shard_map/ppermute | solution.py:300
  68.3 1.5 collective-permute-start.5
  69.8 1.4 collective-permute-start.18
  71.2 5.3 %collective-permute-done.8 = bf16[104,1280]{1,0:T(8,128)(2,1)S(1)} collective-permute-done((bf16[104,1280]{1,0:T(8,128)(2,1)S(1)}, bf16[104,1280]{1,0:T(8,128)(2,1)S(1)}, u32[]{:S(2)}, u32[]{:S(2)}) %collective-permute-start.8) | collective-permute-done | bytes 266272 | tf_op jit(solution)/shard_map/ppermute | solution.py:300
  77.0 3.0 %collective-permute-done.18 = bf16[104,1152]{1,0:T(8,128)(2,1)S(1)} collective-permute-done((bf16[104,1152]{1,0:T(8,128)(2,1)S(1)}, bf16[104,1152]{1,0:T(8,128)(2,1)S(1)}, u32[]{:S(2)}, u32[]{:S(2)}) %collective-permute-start.18) | collective-permute-done | bytes 239648 | tf_op jit(solution)/shard_map/ppermute | solution.py:300
  80.5 2.4 %collective-permute-done.9 = bf16[104,1280]{1,0:T(8,128)(2,1)S(1)} collective-permute-done((bf16[104,1280]{1,0:T(8,128)(2,1)S(1)}, bf16[104,1280]{1,0:T(8,128)(2,1)S(1)}, u32[]{:S(2)}, u32[]{:S(2)}) %collective-permute-start.9) | collective-permute-done | bytes 266272 | tf_op jit(solution)/shard_map/ppermute | solution.py:300
  83.3 2.1 %collective-permute-done.19 = bf16[104,1152]{1,0:T(8,128)(2,1)S(1)} collective-permute-done((bf16[104,1152]{1,0:T(8,128)(2,1)S(1)}, bf16[104,1152]{1,0:T(8,128)(2,1)S(1)}, u32[]{:S(2)}, u32[]{:S(2)}) %collective-permute-start.19) | collective-permute-done | bytes 239648 | tf_op jit(solution)/shard_map/ppermute | solution.py:304
  85.6 3.0 %collective-permute-done.10 = bf16[104,1280]{1,0:T(8,128)(2,1)S(1)} collective-permute-done((bf16[104,1280]{1,0:T(8,128)(2,1)S(1)}, bf16[104,1280]{1,0:T(8,128)(2,1)S(1)}, u32[]{:S(2)}, u32[]{:S(2)}) %collective-permute-start.10) | collective-permute-done | bytes 266272 | tf_op jit(solution)/shard_map/ppermute | solution.py:304
  89.3 3.1 %collective-permute-start.21 = (bf16[72,2432]{1,0:T(8,128)(2,1)S(1)}, bf16[72,2432]{1,0:T(8,128)(2,1)S(1)}, u32[]{:S(2)}, u32[]{:S(2)}) collective-permute-start(bf16[72,2432]{1,0:T(8,128)(2,1)S(1)} %maximum_maximum_fusion.refs_0_), channel_id=1, source_target_pairs={{0,14},{1,15},{2,0},{3,1},{4,2},{5,3},{6,4},{7,5},{8,6},{9,7},{10,... | collective-permute-start | bytes 1050632 | tf_op jit(solution)/shard_map/ppermute | solution.py:300
  92.3 1.3 outward.5.refs_0_
  93.7 3.3 %collective-permute-done.20.refs_0_ = bf16[72,2432]{1,0:T(8,128)(2,1)S(1)} collective-permute-done((bf16[72,2432]{1,0:T(8,128)(2,1)S(1)}, bf16[72,2432]{1,0:T(8,128)(2,1)S(1)}, u32[]{:S(2)}, u32[]{:S(2)}) %collective-permute-start.20) | collective-permute-done | bytes 350240 | tf_op jit(solution)/shard_map/ppermute | solution.py:300
  96.9 3.2 %collective-permute-done.21.refs_1_ = bf16[72,2432]{1,0:T(8,128)(2,1)S(1)} collective-permute-done((bf16[72,2432]{1,0:T(8,128)(2,1)S(1)}, bf16[72,2432]{1,0:T(8,128)(2,1)S(1)}, u32[]{:S(2)}, u32[]{:S(2)}) %collective-permute-start.21) | collective-permute-done | bytes 350240 | tf_op jit(solution)/shard_map/ppermute | solution.py:300
  100.9 2.0 %collective-permute-start.23 = (bf16[72,2432]{1,0:T(8,128)(2,1)S(1)}, bf16[72,2432]{1,0:T(8,128)(2,1)S(1)}, u32[]{:S(2)}, u32[]{:S(2)}) collective-permute-start(bf16[72,2432]{1,0:T(8,128)(2,1)S(1)} %collective-permute-done.21.refs_1_), channel_id=1, source_target_pairs={{0,14},{1,15},{2,0},{3,1},{4,2},{5,3},{6,4},{7,5},{8,6},{9,7},{10,... | collective-permute-start | bytes 1050632 | tf_op jit(solution)/shard_map/ppermute | solution.py:300
  102.9 2.7 %outward.6 = (bf16[72,448]{1,0:T(8,128)(2,1)S(1)}, bf16[72,448]{1,0:T(8,128)(2,1)S(1)}) custom-call(bf16[72,2432]{1,0:T(8,128)(2,1)S(1)} %collective-permute-done.20.refs_0_, bf16[72,2432]{1,0:T(8,128)(2,1)S(1)} %collective-permute-done.21.refs_1_, bf16[448,2432]{1,0:T(8,128)(2,1)S(1)} %bitcast.76, bf16[448,2432]{1,0:T(8,128)(2,1)S(1)} %bitcast.82), custom_call_target="tpu_custom_call" | custom-call | flops 627572736 | bytes 4358144 | tf_op jit(solution)/shard_map/outward/pallas_call | solution.py:204
  105.6 2.0 %collective-permute-done.22.refs_0_ = bf16[72,2432]{1,0:T(8,128)(2,1)S(1)} collective-permute-done((bf16[72,2432]{1,0:T(8,128)(2,1)S(1)}, bf16[72,2432]{1,0:T(8,128)(2,1)S(1)}, u32[]{:S(2)}, u32[]{:S(2)}) %collective-permute-start.22) | collective-permute-done | bytes 350240 | tf_op jit(solution)/shard_map/ppermute | solution.py:300
  107.6 1.2 collective-permute-start.24
  108.7 1.5 collective-permute-start.25
  110.2 1.5 collective-permute-start.26
  111.7 2.7 %outward.7 = (bf16[72,448]{1,0:T(8,128)(2,1)S(1)}, bf16[72,448]{1,0:T(8,128)(2,1)S(1)}) custom-call(bf16[72,2432]{1,0:T(8,128)(2,1)S(1)} %collective-permute-done.22.refs_0_, bf16[72,2432]{1,0:T(8,128)(2,1)S(1)} %collective-permute-done.23.refs_1_, bf16[448,2432]{1,0:T(8,128)(2,1)S(1)} %bitcast.77, bf16[448,2432]{1,0:T(8,128)(2,1)S(1)} %bitcast.83), custom_call_target="tpu_custom_call" | custom-call | flops 627572736 | bytes 4358144 | tf_op jit(solution)/shard_map/outward/pallas_call | solution.py:204
  114.4 5.3 %collective-permute-done.26.refs_1_ = bf16[72,448]{1,0:T(8,128)(2,1)S(1)} collective-permute-done((bf16[72,448]{1,0:T(8,128)(2,1)S(1)}, bf16[72,448]{1,0:T(8,128)(2,1)S(1)}, u32[]{:S(2)}, u32[]{:S(2)}) %collective-permute-start.26) | collective-permute-done | bytes 64544 | tf_op jit(solution)/shard_map/ppermute | solution.py:300
  119.8 2.4 %collective-permute-start.29 = (bf16[40,2432]{1,0:T(8,128)(2,1)S(1)}, bf16[40,2432]{1,0:T(8,128)(2,1)S(1)}, u32[]{:S(2)}, u32[]{:S(2)}) collective-permute-start(bf16[40,2432]{1,0:T(8,128)(2,1)S(1)} %slice.103), channel_id=1, source_target_pairs={{0,14},{1,15},{2,0},{3,1},{4,2},{5,3},{6,4},{7,5},{8,6},{9,7},{10,... | collective-permute-start | bytes 583688 | tf_op jit(solution)/shard_map/ppermute | solution.py:300
  122.3 1.7 collective-permute-start.30
  124.7 2.7 %outward.8 = (bf16[72,448]{1,0:T(8,128)(2,1)S(1)}, bf16[72,448]{1,0:T(8,128)(2,1)S(1)}) custom-call(bf16[72,2432]{1,0:T(8,128)(2,1)S(1)} %collective-permute-done.24.refs_0_, bf16[72,2432]{1,0:T(8,128)(2,1)S(1)} %collective-permute-done.25.refs_1_, bf16[448,2432]{1,0:T(8,128)(2,1)S(1)} %bitcast.78, bf16[448,2432]{1,0:T(8,128)(2,1)S(1)} %bitcast.84), custom_call_target="tpu_custom_call" | custom-call | flops 627572736 | bytes 4358144 | tf_op jit(solution)/shard_map/outward/pallas_call | solution.py:204
  127.4 2.5 %collective-permute-start.32 = (bf16[72,448]{1,0:T(8,128)(2,1)S(1)}, bf16[72,448]{1,0:T(8,128)(2,1)S(1)}, u32[]{:S(2)}, u32[]{:S(2)}) collective-permute-start(bf16[72,448]{1,0:T(8,128)(2,1)S(1)} %get-tuple-element.77), channel_id=1, source_target_pairs={{0,10},{1,11},{2,12},{3,13},{4,14},{5,15},{6,0},{7,1},{8,2},{9,3},... | collective-permute-start | bytes 193544 | tf_op jit(solution)/shard_map/ppermute | solution.py:300
  130.0 1.3 collective-permute-start.34
  131.3 1.3 outward.9
  132.6 3.3 %collective-permute-start.33 = (bf16[72,448]{1,0:T(8,128)(2,1)S(1)}, bf16[72,448]{1,0:T(8,128)(2,1)S(1)}, u32[]{:S(2)}, u32[]{:S(2)}) collective-permute-start(bf16[72,448]{1,0:T(8,128)(2,1)S(1)} %outward.9), channel_id=1, source_target_pairs={{0,8},{1,9},{2,10},{3,11},{4,12},{5,13},{6,14},{7,15},{8,0},{9,1},... | collective-permute-start | bytes 193544 | tf_op jit(solution)/shard_map/ppermute | solution.py:300
  135.9 1.8 collective-permute-done.34.refs_5_
  137.7 4.2 %collective-permute-done.33.refs_4_ = bf16[72,448]{1,0:T(8,128)(2,1)S(1)} collective-permute-done((bf16[72,448]{1,0:T(8,128)(2,1)S(1)}, bf16[72,448]{1,0:T(8,128)(2,1)S(1)}, u32[]{:S(2)}, u32[]{:S(2)}) %collective-permute-start.33) | collective-permute-done | bytes 64544 | tf_op jit(solution)/shard_map/ppermute | solution.py:300
  141.9 1.0 settle.1
  143.0 26.3 %collective-permute-start.35 = (bf16[8,24,448]{2,1,0:T(8,128)(2,1)S(1)}, bf16[8,24,448]{2,1,0:T(8,128)(2,1)S(1)}, u32[]{:S(2)}, u32[]{:S(2)}) collective-permute-start(bf16[8,24,448]{2,1,0:T(8,128)(2,1)S(1)} %get-tuple-element.84), channel_id=1, source_target_pairs={{0,240},{1,241},{2,242},{3,243},{4,244},{5,245},{6,246},{7,247},{8... | collective-permute-start | bytes 516104 | tf_op jit(solution)/shard_map/ppermute | solution.py:314
  169.3 5.2 %collective-permute-start.37 = (bf16[8,24,448]{2,1,0:T(8,128)(2,1)S(1)}, bf16[8,24,448]{2,1,0:T(8,128)(2,1)S(1)}, u32[]{:S(2)}, u32[]{:S(2)}) collective-permute-start(bf16[8,24,448]{2,1,0:T(8,128)(2,1)S(1)} %get-tuple-element.86), channel_id=1, source_target_pairs={{0,16},{1,17},{2,18},{3,19},{4,20},{5,21},{6,22},{7,23},{8,24},{9,... | collective-permute-start | bytes 516104 | tf_op jit(solution)/shard_map/ppermute | solution.py:314
  174.5 3.2 %collective-permute-done.36.far_other = bf16[8,24,448]{2,1,0:T(8,128)(2,1)S(1)} collective-permute-done((bf16[8,24,448]{2,1,0:T(8,128)(2,1)S(1)}, bf16[8,24,448]{2,1,0:T(8,128)(2,1)S(1)}, u32[]{:S(2)}, u32[]{:S(2)}) %collective-permute-start.36) | collective-permute-done | bytes 172064 | tf_op jit(solution)/shard_map/ppermute | solution.py:314
  177.7 3.3 %collective-permute-done.38.near_other = bf16[8,24,448]{2,1,0:T(8,128)(2,1)S(1)} collective-permute-done((bf16[8,24,448]{2,1,0:T(8,128)(2,1)S(1)}, bf16[8,24,448]{2,1,0:T(8,128)(2,1)S(1)}, u32[]{:S(2)}, u32[]{:S(2)}) %collective-permute-start.38) | collective-permute-done | bytes 172064 | tf_op jit(solution)/shard_map/ppermute | solution.py:314
  181.0 5.0 %patch.1 = (bf16[128,7168]{1,0:T(8,128)(2,1)}, bf16[128,7168]{1,0:T(8,128)(2,1)}) custom-call(s32[3]{0:T(128)S(1)} %pad_add_fusion.place, bf16[128,7168]{1,0:T(8,128)(2,1)} %collective-permute-done.fraw, bf16[128,7168]{1,0:T(8,128)(2,1)} %collective-permute-done.1.braw, bf16[8,24,448]{2,1,0:T(8,128)(2,1)S(1)} %collective-permute-done.35.far, ...), custom_call_target="tpu_custom_call" | custom-call | tf_op jit(solution)/shard_map/patch/pallas_call | solution.py:287
  (78 shorter events, 7.9 us)
Async XLA Ops:
  0.6 36.3 %copy-start = (bf16[1,448,2432]{2,1,0:T(8,128)(2,1)S(1)}, bf16[1,448,2432]{2,1,0:T(8,128)(2,1)}, u32[]{:S(2)}) copy-start(bf16[1,448,2432]{2,1,0:T(8,128)(2,1)} %param.16) | copy-start | bytes 6537220
  5.6 38.0 %collective-permute-start = (bf16[128,7168]{1,0:T(8,128)(2,1)}, bf16[128,7168]{1,0:T(8,128)(2,1)}, u32[]{:S(2)}, u32[]{:S(2)}) collective-permute-start(bf16[128,7168]{1,0:T(8,128)(2,1)} %bitcast.88), channel_id=1, source_target_pairs={{0,16},{1,17},{2,18},{3,19},{4,20},{5,21},{6,22},{7,23},{8,24},{9,... | collective-permute-start | bytes 5505032 | tf_op jit(solution)/shard_map/ppermute | solution.py:314
  8.4 35.3 %collective-permute-start.1 = (bf16[128,7168]{1,0:T(8,128)(2,1)}, bf16[128,7168]{1,0:T(8,128)(2,1)}, u32[]{:S(2)}, u32[]{:S(2)}) collective-permute-start(bf16[128,7168]{1,0:T(8,128)(2,1)} %bitcast.90), channel_id=1, source_target_pairs={{0,240},{1,241},{2,242},{3,243},{4,244},{5,245},{6,246},{7,247},{8... | collective-permute-start | bytes 5505032 | tf_op jit(solution)/shard_map/ppermute | solution.py:314
  9.1 27.8 %all-to-all-start = ((bf16[16,56,448]{2,1,0:T(8,128)(2,1)}), bf16[16,56,448]{2,1,0:T(8,128)(2,1)S(1)}, u32[]{:S(2)}, u32[]{:S(2)}) async-start(bf16[16,56,448]{2,1,0:T(8,128)(2,1)} %get-tuple-element.47), calls=%async_computation | async-start | bytes 1835008 | tf_op jit(solution)/shard_map/all_to_all | solution.py:392
  36.9 1.6 copy-start.1
  43.7 5.5 %collective-permute-start.11 = (bf16[48,1152]{1,0:T(8,128)(2,1)S(1)}, bf16[48,1152]{1,0:T(8,128)(2,1)S(1)}, u32[]{:S(2)}, u32[]{:S(2)}) collective-permute-start(bf16[48,1152]{1,0:T(8,128)(2,1)S(1)} %get-tuple-element.63), channel_id=1, source_target_pairs={{0,2},{1,3},{2,4},{3,5},{4,6},{5,7},{6,8},{7,9},{8,10},{9,11},{10,... | collective-permute-start | bytes 331784 | tf_op jit(solution)/shard_map/ppermute | solution.py:300
  44.0 7.7 %collective-permute-start.15 = (bf16[56,1152]{1,0:T(8,128)(2,1)S(1)}, bf16[56,1152]{1,0:T(8,128)(2,1)S(1)}, u32[]{:S(2)}, u32[]{:S(2)}) collective-permute-start(bf16[56,1152]{1,0:T(8,128)(2,1)S(1)} %get-tuple-element.64), channel_id=1, source_target_pairs={{0,14},{1,15},{2,0},{3,1},{4,2},{5,3},{6,4},{7,5},{8,6},{9,7},{10,... | collective-permute-start | bytes 387080 | tf_op jit(solution)/shard_map/ppermute | solution.py:300
  46.6 4.9 %collective-permute-start.2 = (bf16[48,1280]{1,0:T(8,128)(2,1)S(1)}, bf16[48,1280]{1,0:T(8,128)(2,1)S(1)}, u32[]{:S(2)}, u32[]{:S(2)}) collective-permute-start(bf16[48,1280]{1,0:T(8,128)(2,1)S(1)} %get-tuple-element.60), channel_id=1, source_target_pairs={{0,2},{1,3},{2,4},{3,5},{4,6},{5,7},{6,8},{7,9},{8,10},{9,11},{10,... | collective-permute-start | bytes 368648 | tf_op jit(solution)/shard_map/ppermute | solution.py:300
  46.6 7.9 %collective-permute-start.6 = (bf16[56,1280]{1,0:T(8,128)(2,1)S(1)}, bf16[56,1280]{1,0:T(8,128)(2,1)S(1)}, u32[]{:S(2)}, u32[]{:S(2)}) collective-permute-start(bf16[56,1280]{1,0:T(8,128)(2,1)S(1)} %get-tuple-element.61), channel_id=1, source_target_pairs={{0,14},{1,15},{2,0},{3,1},{4,2},{5,3},{6,4},{7,5},{8,6},{9,7},{10,... | collective-permute-start | bytes 430088 | tf_op jit(solution)/shard_map/ppermute | solution.py:300
  49.3 6.3 %collective-permute-start.12 = (bf16[104,1152]{1,0:T(8,128)(2,1)S(1)}, bf16[104,1152]{1,0:T(8,128)(2,1)S(1)}, u32[]{:S(2)}, u32[]{:S(2)}) collective-permute-start(bf16[104,1152]{1,0:T(8,128)(2,1)S(1)} %pad_maximum_fusion.3), channel_id=1, source_target_pairs={{0,2},{1,3},{2,4},{3,5},{4,6},{5,7},{6,8},{7,9},{8,10},{9,11},{10,... | collective-permute-start | bytes 718856 | tf_op jit(solution)/shard_map/ppermute | solution.py:300
  51.6 6.9 %collective-permute-start.3 = (bf16[104,1280]{1,0:T(8,128)(2,1)S(1)}, bf16[104,1280]{1,0:T(8,128)(2,1)S(1)}, u32[]{:S(2)}, u32[]{:S(2)}) collective-permute-start(bf16[104,1280]{1,0:T(8,128)(2,1)S(1)} %pad_maximum_fusion.1), channel_id=1, source_target_pairs={{0,2},{1,3},{2,4},{3,5},{4,6},{5,7},{6,8},{7,9},{8,10},{9,11},{10,... | collective-permute-start | bytes 798728 | tf_op jit(solution)/shard_map/ppermute | solution.py:300
  51.8 6.9 %collective-permute-start.16 = (bf16[104,1152]{1,0:T(8,128)(2,1)S(1)}, bf16[104,1152]{1,0:T(8,128)(2,1)S(1)}, u32[]{:S(2)}, u32[]{:S(2)}) collective-permute-start(bf16[104,1152]{1,0:T(8,128)(2,1)S(1)} %pad_maximum_fusion.4), channel_id=1, source_target_pairs={{0,14},{1,15},{2,0},{3,1},{4,2},{5,3},{6,4},{7,5},{8,6},{9,7},{10,... | collective-permute-start | bytes 718856 | tf_op jit(solution)/shard_map/ppermute | solution.py:300
  54.6 10.6 %collective-permute-start.7 = (bf16[104,1280]{1,0:T(8,128)(2,1)S(1)}, bf16[104,1280]{1,0:T(8,128)(2,1)S(1)}, u32[]{:S(2)}, u32[]{:S(2)}) collective-permute-start(bf16[104,1280]{1,0:T(8,128)(2,1)S(1)} %pad_maximum_fusion.2), channel_id=1, source_target_pairs={{0,14},{1,15},{2,0},{3,1},{4,2},{5,3},{6,4},{7,5},{8,6},{9,7},{10,... | collective-permute-start | bytes 798728 | tf_op jit(solution)/shard_map/ppermute | solution.py:300
  55.7 7.6 %collective-permute-start.13 = (bf16[104,1152]{1,0:T(8,128)(2,1)S(1)}, bf16[104,1152]{1,0:T(8,128)(2,1)S(1)}, u32[]{:S(2)}, u32[]{:S(2)}) collective-permute-start(bf16[104,1152]{1,0:T(8,128)(2,1)S(1)} %fusion.8), channel_id=1, source_target_pairs={{0,2},{1,3},{2,4},{3,5},{4,6},{5,7},{6,8},{7,9},{8,10},{9,11},{10,... | collective-permute-start | bytes 718856 | tf_op jit(solution)/shard_map/ppermute | solution.py:300
  58.5 9.5 %collective-permute-start.4 = (bf16[104,1280]{1,0:T(8,128)(2,1)S(1)}, bf16[104,1280]{1,0:T(8,128)(2,1)S(1)}, u32[]{:S(2)}, u32[]{:S(2)}) collective-permute-start(bf16[104,1280]{1,0:T(8,128)(2,1)S(1)} %fusion.2), channel_id=1, source_target_pairs={{0,2},{1,3},{2,4},{3,5},{4,6},{5,7},{6,8},{7,9},{8,10},{9,11},{10,... | collective-permute-start | bytes 798728 | tf_op jit(solution)/shard_map/ppermute | solution.py:300
  63.4 6.3 %collective-permute-start.17 = (bf16[104,1152]{1,0:T(8,128)(2,1)S(1)}, bf16[104,1152]{1,0:T(8,128)(2,1)S(1)}, u32[]{:S(2)}, u32[]{:S(2)}) collective-permute-start(bf16[104,1152]{1,0:T(8,128)(2,1)S(1)} %get-tuple-element.93), channel_id=1, source_target_pairs={{0,14},{1,15},{2,0},{3,1},{4,2},{5,3},{6,4},{7,5},{8,6},{9,7},{10,... | collective-permute-start | bytes 718856 | tf_op jit(solution)/shard_map/ppermute | solution.py:300
  63.7 13.3 %collective-permute-start.14 = (bf16[104,1152]{1,0:T(8,128)(2,1)S(1)}, bf16[104,1152]{1,0:T(8,128)(2,1)S(1)}, u32[]{:S(2)}, u32[]{:S(2)}) collective-permute-start(bf16[104,1152]{1,0:T(8,128)(2,1)S(1)} %get-tuple-element.92), channel_id=1, source_target_pairs={{0,2},{1,3},{2,4},{3,5},{4,6},{5,7},{6,8},{7,9},{8,10},{9,11},{10,... | collective-permute-start | bytes 718856 | tf_op jit(solution)/shard_map/ppermute | solution.py:300
  68.2 8.3 %collective-permute-start.8 = (bf16[104,1280]{1,0:T(8,128)(2,1)S(1)}, bf16[104,1280]{1,0:T(8,128)(2,1)S(1)}, u32[]{:S(2)}, u32[]{:S(2)}) collective-permute-start(bf16[104,1280]{1,0:T(8,128)(2,1)S(1)} %get-tuple-element.91), channel_id=1, source_target_pairs={{0,14},{1,15},{2,0},{3,1},{4,2},{5,3},{6,4},{7,5},{8,6},{9,7},{10,... | collective-permute-start | bytes 798728 | tf_op jit(solution)/shard_map/ppermute | solution.py:300
  68.3 12.2 %collective-permute-start.5 = (bf16[104,1280]{1,0:T(8,128)(2,1)S(1)}, bf16[104,1280]{1,0:T(8,128)(2,1)S(1)}, u32[]{:S(2)}, u32[]{:S(2)}) collective-permute-start(bf16[104,1280]{1,0:T(8,128)(2,1)S(1)} %get-tuple-element.90), channel_id=1, source_target_pairs={{0,2},{1,3},{2,4},{3,5},{4,6},{5,7},{6,8},{7,9},{8,10},{9,11},{10,... | collective-permute-start | bytes 798728 | tf_op jit(solution)/shard_map/ppermute | solution.py:300
  69.8 10.1 %collective-permute-start.18 = (bf16[104,1152]{1,0:T(8,128)(2,1)S(1)}, bf16[104,1152]{1,0:T(8,128)(2,1)S(1)}, u32[]{:S(2)}, u32[]{:S(2)}) collective-permute-start(bf16[104,1152]{1,0:T(8,128)(2,1)S(1)} %fusion.7), channel_id=1, source_target_pairs={{0,14},{1,15},{2,0},{3,1},{4,2},{5,3},{6,4},{7,5},{8,6},{9,7},{10,... | collective-permute-start | bytes 718856 | tf_op jit(solution)/shard_map/ppermute | solution.py:300
  76.6 6.2 %collective-permute-start.9 = (bf16[104,1280]{1,0:T(8,128)(2,1)S(1)}, bf16[104,1280]{1,0:T(8,128)(2,1)S(1)}, u32[]{:S(2)}, u32[]{:S(2)}) collective-permute-start(bf16[104,1280]{1,0:T(8,128)(2,1)S(1)} %fusion.1), channel_id=1, source_target_pairs={{0,14},{1,15},{2,0},{3,1},{4,2},{5,3},{6,4},{7,5},{8,6},{9,7},{10,... | collective-permute-start | bytes 798728 | tf_op jit(solution)/shard_map/ppermute | solution.py:300
  80.1 5.4 %collective-permute-start.19 = (bf16[104,1152]{1,0:T(8,128)(2,1)S(1)}, bf16[104,1152]{1,0:T(8,128)(2,1)S(1)}, u32[]{:S(2)}, u32[]{:S(2)}) collective-permute-start(bf16[104,1152]{1,0:T(8,128)(2,1)S(1)} %fusion.11), channel_id=1, source_target_pairs={{0,1},{1,0},{2,3},{3,2},{4,5},{5,4},{6,7},{7,6},{8,9},{9,8},{10,11... | collective-permute-start | bytes 718856 | tf_op jit(solution)/shard_map/ppermute | solution.py:304
  82.9 5.6 %collective-permute-start.10 = (bf16[104,1280]{1,0:T(8,128)(2,1)S(1)}, bf16[104,1280]{1,0:T(8,128)(2,1)S(1)}, u32[]{:S(2)}, u32[]{:S(2)}) collective-permute-start(bf16[104,1280]{1,0:T(8,128)(2,1)S(1)} %fusion.5), channel_id=1, source_target_pairs={{0,1},{1,0},{2,3},{3,2},{4,5},{5,4},{6,7},{7,6},{8,9},{9,8},{10,11... | collective-permute-start | bytes 798728 | tf_op jit(solution)/shard_map/ppermute | solution.py:304
  88.9 8.1 %collective-permute-start.20 = (bf16[72,2432]{1,0:T(8,128)(2,1)S(1)}, bf16[72,2432]{1,0:T(8,128)(2,1)S(1)}, u32[]{:S(2)}, u32[]{:S(2)}) collective-permute-start(bf16[72,2432]{1,0:T(8,128)(2,1)S(1)} %maximum_maximum_fusion.refs_0_), channel_id=1, source_target_pairs={{0,2},{1,3},{2,4},{3,5},{4,6},{5,7},{6,8},{7,9},{8,10},{9,11},{10,... | collective-permute-start | bytes 1050632 | tf_op jit(solution)/shard_map/ppermute | solution.py:300
  89.3 10.9 %collective-permute-start.21 = (bf16[72,2432]{1,0:T(8,128)(2,1)S(1)}, bf16[72,2432]{1,0:T(8,128)(2,1)S(1)}, u32[]{:S(2)}, u32[]{:S(2)}) collective-permute-start(bf16[72,2432]{1,0:T(8,128)(2,1)S(1)} %maximum_maximum_fusion.refs_0_), channel_id=1, source_target_pairs={{0,14},{1,15},{2,0},{3,1},{4,2},{5,3},{6,4},{7,5},{8,6},{9,7},{10,... | collective-permute-start | bytes 1050632 | tf_op jit(solution)/shard_map/ppermute | solution.py:300
  100.2 7.4 %collective-permute-start.22 = (bf16[72,2432]{1,0:T(8,128)(2,1)S(1)}, bf16[72,2432]{1,0:T(8,128)(2,1)S(1)}, u32[]{:S(2)}, u32[]{:S(2)}) collective-permute-start(bf16[72,2432]{1,0:T(8,128)(2,1)S(1)} %collective-permute-done.20.refs_0_), channel_id=1, source_target_pairs={{0,2},{1,3},{2,4},{3,5},{4,6},{5,7},{6,8},{7,9},{8,10},{9,11},{10,... | collective-permute-start | bytes 1050632 | tf_op jit(solution)/shard_map/ppermute | solution.py:300
  100.9 6.7 %collective-permute-start.23 = (bf16[72,2432]{1,0:T(8,128)(2,1)S(1)}, bf16[72,2432]{1,0:T(8,128)(2,1)S(1)}, u32[]{:S(2)}, u32[]{:S(2)}) collective-permute-start(bf16[72,2432]{1,0:T(8,128)(2,1)S(1)} %collective-permute-done.21.refs_1_), channel_id=1, source_target_pairs={{0,14},{1,15},{2,0},{3,1},{4,2},{5,3},{6,4},{7,5},{8,6},{9,7},{10,... | collective-permute-start | bytes 1050632 | tf_op jit(solution)/shard_map/ppermute | solution.py:300
  107.6 12.2 %collective-permute-start.24 = (bf16[72,2432]{1,0:T(8,128)(2,1)S(1)}, bf16[72,2432]{1,0:T(8,128)(2,1)S(1)}, u32[]{:S(2)}, u32[]{:S(2)}) collective-permute-start(bf16[72,2432]{1,0:T(8,128)(2,1)S(1)} %collective-permute-done.22.refs_0_), channel_id=1, source_target_pairs={{0,2},{1,3},{2,4},{3,5},{4,6},{5,7},{6,8},{7,9},{8,10},{9,11},{10,... | collective-permute-start | bytes 1050632 | tf_op jit(solution)/shard_map/ppermute | solution.py:300
  108.7 11.0 %collective-permute-start.25 = (bf16[72,2432]{1,0:T(8,128)(2,1)S(1)}, bf16[72,2432]{1,0:T(8,128)(2,1)S(1)}, u32[]{:S(2)}, u32[]{:S(2)}) collective-permute-start(bf16[72,2432]{1,0:T(8,128)(2,1)S(1)} %collective-permute-done.23.refs_1_), channel_id=1, source_target_pairs={{0,14},{1,15},{2,0},{3,1},{4,2},{5,3},{6,4},{7,5},{8,6},{9,7},{10,... | collective-permute-start | bytes 1050632 | tf_op jit(solution)/shard_map/ppermute | solution.py:300
  110.2 9.5 %collective-permute-start.26 = (bf16[72,448]{1,0:T(8,128)(2,1)S(1)}, bf16[72,448]{1,0:T(8,128)(2,1)S(1)}, u32[]{:S(2)}, u32[]{:S(2)}) collective-permute-start(bf16[72,448]{1,0:T(8,128)(2,1)S(1)} %get-tuple-element.68), channel_id=1, source_target_pairs={{0,14},{1,15},{2,0},{3,1},{4,2},{5,3},{6,4},{7,5},{8,6},{9,7},{10,... | collective-permute-start | bytes 193544 | tf_op jit(solution)/shard_map/ppermute | solution.py:300
  111.7 8.0 %collective-permute-start.27 = (bf16[72,448]{1,0:T(8,128)(2,1)S(1)}, bf16[72,448]{1,0:T(8,128)(2,1)S(1)}, u32[]{:S(2)}, u32[]{:S(2)}) collective-permute-start(bf16[72,448]{1,0:T(8,128)(2,1)S(1)} %get-tuple-element.69), channel_id=1, source_target_pairs={{0,2},{1,3},{2,4},{3,5},{4,6},{5,7},{6,8},{7,9},{8,10},{9,11},{10,... | collective-permute-start | bytes 193544 | tf_op jit(solution)/shard_map/ppermute | solution.py:300
  119.8 11.5 %collective-permute-start.29 = (bf16[40,2432]{1,0:T(8,128)(2,1)S(1)}, bf16[40,2432]{1,0:T(8,128)(2,1)S(1)}, u32[]{:S(2)}, u32[]{:S(2)}) collective-permute-start(bf16[40,2432]{1,0:T(8,128)(2,1)S(1)} %slice.103), channel_id=1, source_target_pairs={{0,14},{1,15},{2,0},{3,1},{4,2},{5,3},{6,4},{7,5},{8,6},{9,7},{10,... | collective-permute-start | bytes 583688 | tf_op jit(solution)/shard_map/ppermute | solution.py:300
  122.2 9.0 %collective-permute-start.28 = (bf16[32,2432]{1,0:T(8,128)(2,1)S(1)}, bf16[32,2432]{1,0:T(8,128)(2,1)S(1)}, u32[]{:S(2)}, u32[]{:S(2)}) collective-permute-start(bf16[32,2432]{1,0:T(8,128)(2,1)S(1)} %slice.102), channel_id=1, source_target_pairs={{0,2},{1,3},{2,4},{3,5},{4,6},{5,7},{6,8},{7,9},{8,10},{9,11},{10,... | collective-permute-start | bytes 466952 | tf_op jit(solution)/shard_map/ppermute | solution.py:300
  122.3 7.7 %collective-permute-start.30 = (bf16[72,448]{1,0:T(8,128)(2,1)S(1)}, bf16[72,448]{1,0:T(8,128)(2,1)S(1)}, u32[]{:S(2)}, u32[]{:S(2)}) collective-permute-start(bf16[72,448]{1,0:T(8,128)(2,1)S(1)} %get-tuple-element.72), channel_id=1, source_target_pairs={{0,12},{1,13},{2,14},{3,15},{4,0},{5,1},{6,2},{7,3},{8,4},{9,5},{1... | collective-permute-start | bytes 193544 | tf_op jit(solution)/shard_map/ppermute | solution.py:300
  124.0 7.2 %collective-permute-start.31 = (bf16[72,448]{1,0:T(8,128)(2,1)S(1)}, bf16[72,448]{1,0:T(8,128)(2,1)S(1)}, u32[]{:S(2)}, u32[]{:S(2)}) collective-permute-start(bf16[72,448]{1,0:T(8,128)(2,1)S(1)} %get-tuple-element.73), channel_id=1, source_target_pairs={{0,4},{1,5},{2,6},{3,7},{4,8},{5,9},{6,10},{7,11},{8,12},{9,13},{1... | collective-permute-start | bytes 193544 | tf_op jit(solution)/shard_map/ppermute | solution.py:300
  127.4 8.5 %collective-permute-start.32 = (bf16[72,448]{1,0:T(8,128)(2,1)S(1)}, bf16[72,448]{1,0:T(8,128)(2,1)S(1)}, u32[]{:S(2)}, u32[]{:S(2)}) collective-permute-start(bf16[72,448]{1,0:T(8,128)(2,1)S(1)} %get-tuple-element.77), channel_id=1, source_target_pairs={{0,10},{1,11},{2,12},{3,13},{4,14},{5,15},{6,0},{7,1},{8,2},{9,3},... | collective-permute-start | bytes 193544 | tf_op jit(solution)/shard_map/ppermute | solution.py:300
  130.0 7.8 %collective-permute-start.34 = (bf16[72,448]{1,0:T(8,128)(2,1)S(1)}, bf16[72,448]{1,0:T(8,128)(2,1)S(1)}, u32[]{:S(2)}, u32[]{:S(2)}) collective-permute-start(bf16[72,448]{1,0:T(8,128)(2,1)S(1)} %get-tuple-element.78), channel_id=1, source_target_pairs={{0,6},{1,7},{2,8},{3,9},{4,10},{5,11},{6,12},{7,13},{8,14},{9,15},... | collective-permute-start | bytes 193544 | tf_op jit(solution)/shard_map/ppermute | solution.py:300
  131.3 10.6 %copy-start.2 = (f32[8,128]{1,0:T(8,128)S(1)}, f32[8,128]{1,0:T(8,128)}, u32[]{:S(2)}) copy-start(f32[8,128]{1,0:T(8,128)} %get-tuple-element.58.meta) | copy-start | bytes 12292
  132.6 9.3 %collective-permute-start.33 = (bf16[72,448]{1,0:T(8,128)(2,1)S(1)}, bf16[72,448]{1,0:T(8,128)(2,1)S(1)}, u32[]{:S(2)}, u32[]{:S(2)}) collective-permute-start(bf16[72,448]{1,0:T(8,128)(2,1)S(1)} %outward.9), channel_id=1, source_target_pairs={{0,8},{1,9},{2,10},{3,11},{4,12},{5,13},{6,14},{7,15},{8,0},{9,1},... | collective-permute-start | bytes 193544 | tf_op jit(solution)/shard_map/ppermute | solution.py:300
  143.0 31.5 %collective-permute-start.35 = (bf16[8,24,448]{2,1,0:T(8,128)(2,1)S(1)}, bf16[8,24,448]{2,1,0:T(8,128)(2,1)S(1)}, u32[]{:S(2)}, u32[]{:S(2)}) collective-permute-start(bf16[8,24,448]{2,1,0:T(8,128)(2,1)S(1)} %get-tuple-element.84), channel_id=1, source_target_pairs={{0,240},{1,241},{2,242},{3,243},{4,244},{5,245},{6,246},{7,247},{8... | collective-permute-start | bytes 516104 | tf_op jit(solution)/shard_map/ppermute | solution.py:314
  169.3 8.4 %collective-permute-start.36 = (bf16[8,24,448]{2,1,0:T(8,128)(2,1)S(1)}, bf16[8,24,448]{2,1,0:T(8,128)(2,1)S(1)}, u32[]{:S(2)}, u32[]{:S(2)}) collective-permute-start(bf16[8,24,448]{2,1,0:T(8,128)(2,1)S(1)} %get-tuple-element.85), channel_id=1, source_target_pairs={{0,241},{1,240},{2,243},{3,242},{4,245},{5,244},{6,247},{7,246},{8... | collective-permute-start | bytes 516104 | tf_op jit(solution)/shard_map/ppermute | solution.py:314
  169.3 8.3 %collective-permute-start.37 = (bf16[8,24,448]{2,1,0:T(8,128)(2,1)S(1)}, bf16[8,24,448]{2,1,0:T(8,128)(2,1)S(1)}, u32[]{:S(2)}, u32[]{:S(2)}) collective-permute-start(bf16[8,24,448]{2,1,0:T(8,128)(2,1)S(1)} %get-tuple-element.86), channel_id=1, source_target_pairs={{0,16},{1,17},{2,18},{3,19},{4,20},{5,21},{6,22},{7,23},{8,24},{9,... | collective-permute-start | bytes 516104 | tf_op jit(solution)/shard_map/ppermute | solution.py:314
  174.5 6.5 %collective-permute-start.38 = (bf16[8,24,448]{2,1,0:T(8,128)(2,1)S(1)}, bf16[8,24,448]{2,1,0:T(8,128)(2,1)S(1)}, u32[]{:S(2)}, u32[]{:S(2)}) collective-permute-start(bf16[8,24,448]{2,1,0:T(8,128)(2,1)S(1)} %get-tuple-element.87), channel_id=1, source_target_pairs={{0,17},{1,16},{2,19},{3,18},{4,21},{5,20},{6,23},{7,22},{8,25},{9,... | collective-permute-start | bytes 516104 | tf_op jit(solution)/shard_map/ppermute | solution.py:314
